TPU v7x, 512 devices: a whole 4x4x16 slice. The times are simulated.
512 devices in a mesh: band: 32 (over z, core), col: 16 (over y, x).
Axes of the slice: x: 4, y: 4, z: 16, core: 2. Of those that a mesh axis runs over, the one named last changes fastest.
Arguments:
- atm_state: bfloat16 [128, 1440, 384], P('band', 'col'), may hold values from -6 to 6
- spec_gain: float32 [2, 720, 384], P(None, None, 'col'), may hold values from -4 to 4
- mlp_in: bfloat16 [384, 768], replicated, may hold values from -0.3125 to 0.3125
- mlp_out: bfloat16 [768, 384], replicated, may hold values from -0.21875 to 0.21875
- flux_proj: bfloat16 [384, 16], replicated, may hold values from -0.3125 to 0.3125
- pair_rows: int32 [32, 32, 4], P(None, 'band'), may hold values from 0 to 3, as said below
- pair_count: int32 [32, 32], P(None, 'band'), may hold values from 0 to 4, as said below
- pair_weight: float32 [192, 32, 4], P('band'), may hold values from 0.05 to 1
- ocean_state: bfloat16 [192, 1440, 200], P('band', 'col'), may hold values from -6 to 6
- force_proj: bfloat16 [16, 200], replicated, may hold values from -1.5 to 1.5
- depth_kernel: float32 [7, 7, 200], replicated, may hold values from -0.875 to 0.875
- ocean_in: bfloat16 [200, 800], replicated, may hold values from -0.4375 to 0.4375
- ocean_out: bfloat16 [800, 200], replicated, may hold values from -0.21875 to 0.21875
- surf_proj: bfloat16 [200, 16], replicated, may hold values from -0.4375 to 0.4375
- land_mask: int32 [192, 1440], P('band', 'col'), may hold values 0 or 1
Outputs:
- atm_next: bfloat16 [128, 1440, 384], P('band', 'col')
- ocean_next: bfloat16 [192, 1440, 200], P('band', 'col')
- atm_surface: bfloat16 [128, 1440, 16], P('band', 'col')
Inputs may be any that keep to these rules, and one draw needn't show every extreme that they name: `pair_rows`: for each pair, 4 distinct local row numbers of the atmosphere band; only the first pair_count of them are used. pair_count[r, s] is 0 unless 0 <= s - r < 4; in every draw some pair uses all 4 slots.
All inputs are finite; a program needn't handle non-finite values. No bound on the sum of `land_mask` on one device may be relied on, other than what follows from the above.
Results may differ from a plain program's by a relative error of at most 0.02.
Values may be sent and summed in bfloat16 or wider, within the bound.
A program may use at most 64 MiB of HBM per device.

v0:
```python
import jax
import jax.numpy as jnp
from jax import lax
from jax.sharding import PartitionSpec as P

SPAN = 4


HIGH = lax.Precision.HIGHEST
FAIR = lax.Precision.HIGH


def passed_along(value, axis, by):
    size = lax.axis_size(axis)
    pairs = [(i, i + by) for i in range(size) if 0 <= i + by < size]
    return lax.ppermute(value, axis, pairs)


def with_halo(value, sides, width):
    for axis, dim in sides:
        size, length = (lax.axis_size(axis), value.shape[dim])
        up = [(i, (i + 1) % size) for i in range(size)]
        down = [(j, i) for i, j in up]
        last = lax.slice_in_dim(value, length - width, length, axis=dim)
        initial = lax.slice_in_dim(value, 0, width, axis=dim)
        before = lax.ppermute(last, axis, up)
        after = lax.ppermute(initial, axis, down)
        value = jnp.concatenate([before, value, after], axis=dim)
    return value


def layer_norm(values):
    mean = jnp.mean(values, axis=-1, keepdims=True)
    centred = values - mean
    spread = jnp.mean(centred * centred, axis=-1, keepdims=True)
    return centred * lax.rsqrt(spread + 1e-05)


def wave_table(count, length):
    order = jnp.arange(count, dtype=jnp.int32)[:, None]
    place = jnp.arange(length, dtype=jnp.int32)[None, :]
    phase = order * place % length
    angle = 2.0 * jnp.pi / length * phase.astype(jnp.float32)
    return jnp.concatenate([jnp.cos(angle), jnp.sin(angle)], axis=0)


def per_device(
    atm_state,
    spec_gain,
    mlp_in,
    mlp_out,
    flux_proj,
    pair_rows,
    pair_count,
    pair_weight,
    ocean_state,
    force_proj,
    depth_kernel,
    ocean_in,
    ocean_out,
    surf_proj,
    land_mask,
):
    band_count = lax.axis_size("band")
    band_here = lax.axis_index("band")
    lat_rows, lon_dev, channels = atm_state.shape
    wave_count = spec_gain.shape[1]
    length = lon_dev * lax.axis_size("col")
    table = wave_table(wave_count, length)
    table_high = table.astype(jnp.bfloat16)
    table_low = (table - table_high.astype(jnp.float32)).astype(jnp.bfloat16)
    gain_real = spec_gain[0]
    gain_imag = spec_gain[1]
    latitudes = lax.all_to_all(atm_state, "col", split_axis=2, concat_axis=1, tiled=True)
    spectra = jnp.einsum("kl,alc->akc", table_high, latitudes, preferred_element_type=jnp.float32)
    spectra = spectra + jnp.einsum(
        "kl,alc->akc", table_low, latitudes, preferred_element_type=jnp.float32
    )
    cos_part = spectra[:, :wave_count]
    sin_part = spectra[:, wave_count:]
    new_cos = gain_real * cos_part + gain_imag * sin_part
    new_sin = gain_real * sin_part - gain_imag * cos_part
    filtered = jnp.concatenate([new_cos, new_sin], axis=1)
    zonal = jnp.einsum("kl,akc->alc", table, filtered, precision=FAIR) * (2.0 / length)
    zonal = lax.all_to_all(
        zonal.astype(jnp.bfloat16), "col", split_axis=1, concat_axis=2, tiled=True
    )
    mixed = atm_state.astype(jnp.float32) + zonal.astype(jnp.float32)
    normed = layer_norm(mixed).astype(jnp.bfloat16)
    inner = jax.nn.gelu(jnp.dot(normed, mlp_in, preferred_element_type=jnp.float32)).astype(
        jnp.bfloat16
    )
    atm_next = (mixed + jnp.dot(inner, mlp_out, preferred_element_type=jnp.float32)).astype(
        jnp.bfloat16
    )
    flux = jnp.dot(atm_next, flux_proj, preferred_element_type=jnp.float32).astype(jnp.bfloat16)
    rows_here = pair_rows[:, 0, :]
    slot_count = rows_here.shape[1]
    valid = jnp.arange(slot_count, dtype=jnp.int32)[None, :] < pair_count
    latitude_ids = jnp.arange(lat_rows, dtype=jnp.int32)[None, None, :]
    select = ((rows_here[:, :, None] == latitude_ids) & valid[:, :, None]).astype(jnp.bfloat16)
    outgoing = jnp.einsum("rpa,alf->rplf", select, flux, preferred_element_type=jnp.float32).astype(
        jnp.bfloat16
    )
    ocean_rows = ocean_state.shape[0]
    forcing = jnp.zeros((ocean_rows, lon_dev, flux.shape[2]), jnp.float32)
    for offset in range(SPAN):
        sender = jnp.clip(band_here - offset, 0, band_count - 1)
        piece = lax.dynamic_index_in_dim(outgoing, sender, 0, keepdims=False)
        if offset > 0:
            piece = passed_along(piece, "band", -offset)
        source = jnp.clip(band_here + offset, 0, band_count - 1)
        share = lax.dynamic_index_in_dim(pair_weight, source, 1, keepdims=False)
        forcing = forcing + jnp.einsum(
            "ip,plf->ilf", share, piece.astype(jnp.float32), precision=HIGH
        )
    lifted = (
        ocean_state.astype(jnp.float32)
        + jnp.dot(forcing.astype(jnp.bfloat16), force_proj, preferred_element_type=jnp.float32)
    ).astype(jnp.bfloat16)
    rim = depth_kernel.shape[0] // 2
    framed = with_halo(lifted, (("band", 0), ("col", 1)), rim)
    place = jnp.arange(ocean_rows + 2 * rim, dtype=jnp.int32)
    outside = (band_here == 0) & (place < rim) | (band_here == band_count - 1) & (
        place >= ocean_rows + rim
    )
    framed = jnp.where(outside[:, None, None], jnp.zeros((), jnp.bfloat16), framed).astype(
        jnp.float32
    )
    stencil = jnp.zeros(lifted.shape, jnp.float32)
    for down in range(2 * rim + 1):
        for across in range(2 * rim + 1):
            stencil = (
                stencil
                + depth_kernel[down, across]
                * framed[down : down + ocean_rows, across : across + lon_dev]
            )
    onorm = layer_norm(stencil).astype(jnp.bfloat16)
    ohidden = jax.nn.gelu(jnp.dot(onorm, ocean_in, preferred_element_type=jnp.float32)).astype(
        jnp.bfloat16
    )
    sea = land_mask.astype(jnp.float32)
    ocean_next = (
        (
            lifted.astype(jnp.float32)
            + jnp.dot(ohidden, ocean_out, preferred_element_type=jnp.float32)
        )
        * sea[:, :, None]
    ).astype(jnp.bfloat16)
    surface = jnp.dot(ocean_next, surf_proj, preferred_element_type=jnp.float32).astype(
        jnp.bfloat16
    )
    surface_wide = surface.astype(jnp.float32)
    gathered = jnp.zeros((lat_rows, lon_dev, surface.shape[2]), jnp.float32)
    for offset in range(SPAN):
        target = jnp.clip(band_here + offset, 0, band_count - 1)
        share = lax.dynamic_index_in_dim(pair_weight, target, 1, keepdims=False)
        piece = jnp.einsum("ip,ilg->plg", share, surface_wide, precision=HIGH).astype(jnp.bfloat16)
        if offset > 0:
            piece = passed_along(piece, "band", offset)
        anchor = jnp.clip(band_here - offset, 0, band_count - 1)
        chosen = lax.dynamic_index_in_dim(select, anchor, 0, keepdims=False)
        gathered = gathered + jnp.einsum(
            "pa,plg->alg", chosen, piece, preferred_element_type=jnp.float32
        )
    return (atm_next, ocean_next, gathered.astype(jnp.bfloat16))


def solution(mesh):
    placed = (
        P("band", "col", None),
        P(None, None, "col"),
        P(),
        P(),
        P(),
        P(None, "band", None),
        P(None, "band"),
        P("band", None, None),
        P("band", "col", None),
        P(),
        P(),
        P(),
        P(),
        P(),
        P("band", "col"),
    )
    return jax.shard_map(
        per_device,
        mesh=mesh,
        in_specs=placed,
        out_specs=(P("band", "col", None), P("band", "col", None), P("band", "col", None)),
        check_vma=False,
    )
```

profile of v0, /device:TPU:1, one launch (start us, length us, event | category | flops | bytes accessed | tf_op | source)
XLA Modules:
  0.0 118.6 jit_solution(13154964971236712555)
XLA Ops:
  0.6 2.0 %copy.51 = bf16[4,90,384]{1,0,2:T(4,128)(2,1)} copy(bf16[4,90,384]{2,0,1:T(4,128)(2,1)} %param.15) | data formatting | bytes 552960 | tf_op args[0]
  2.7 7.6 %all-to-all-start = ((bf16[4,90,384]{1,0,2:T(4,128)(2,1)}), bf16[4,90,384]{1,0,2:T(4,128)(2,1)S(1)}, u32[]{:S(2)}, u32[]{:S(2)}) async-start(bf16[4,90,384]{1,0,2:T(4,128)(2,1)} %copy.51), calls=%async_computation | async-start | bytes 786432 | tf_op jit(solution)/shard_map/all_to_all | solution.py:74
  10.3 19.6 %fusion.9 = (f32[720,1440]{1,0:T(8,128)}, f32[720,1440]{1,0:T(8,128)}) fusion(), kind=kLoop, calls=%fused_computation.12 | loop fusion | flops 9331200 | bytes 8294400 | tf_op jit(solution)/shard_map/sin | solution.py:44
  30.8 5.2 %fusion.11 = f32[1440,96]{0,1:S(1)} fusion(bf16[1440,96]{0,1:T(8,128)(2,1)S(1)} %bitcast.191, f32[720,1440]{1,0:T(8,128)} %get-tuple-element.79, f32[720,1440]{1,0:T(8,128)} %get-tuple-element.80), kind=kOutput, calls=%fused_computation.14 | convolution fusion | flops 408499200 | bytes 9123840
  37.0 1.5 %fusion.3 = f32[1440,96]{0,1:S(1)} fusion(bf16[1440,96]{0,1:T(8,128)(2,1)S(1)} %bitcast.192, f32[720,1440]{1,0:T(8,128)S(1)} %bitcast.185, f32[720,1440]{1,0:T(8,128)S(1)} %copy-done.1), kind=kOutput, calls=%fused_computation.6 | convolution fusion | flops 406425600 | bytes 9123840
  38.7 2.9 %fusion.19 = bf16[4,1440,24]{1,2,0:T(8,128)(2,1)S(1)} fusion(f32[720,1440]{1,0:T(8,128)S(1)} %bitcast.185, f32[720,1440]{1,0:T(8,128)S(1)} %copy-done.1, f32[4,720,24]{1,2,0:T(8,128)S(1)} %get-tuple-element.15, f32[4,720,24]{1,2,0:T(8,128)S(1)} %get-tuple-element.14), kind=kOutput, calls=%fused_computation.19 | convolution fusion | flops 1196881920 | bytes 9123840 | tf_op jit(solution)/shard_map/kl,akc->alc/dot_general | solution.py:84
  41.7 1.7 %copy.54 = bf16[4,1440,24]{2,0,1:T(4,128)(2,1)S(1)} copy(bf16[4,1440,24]{1,2,0:T(8,128)(2,1)S(1)} %fusion.19) | data formatting | bytes 552960 | tf_op jit(solution)/shard_map/convert_element_type | solution.py:86
  43.4 2.6 %reshape.91 = bf16[16,2,4320]{2,1,0:T(2,128)(2,1)} reshape(bf16[1440,4,24]{2,1,0:T(4,128)(2,1)S(1)} %bitcast.186) | data formatting | bytes 552960
  46.0 6.7 %all-to-all-start.1 = ((bf16[16,2,4320]{2,1,0:T(2,128)(2,1)}), bf16[16,2,4320]{2,1,0:T(2,128)(2,1)S(1)}, u32[]{:S(2)}, u32[]{:S(2)}) async-start(bf16[16,2,4320]{2,1,0:T(2,128)(2,1)} %reshape.91), calls=%async_computation.1 | async-start | bytes 557056 | tf_op jit(solution)/shard_map/all_to_all | solution.py:85
  53.3 6.9 %all-to-all-done.1 = bf16[16,2,4320]{2,1,0:T(2,128)(2,1)S(1)} async-done(((bf16[16,2,4320]{2,1,0:T(2,128)(2,1)}), bf16[16,2,4320]{2,1,0:T(2,128)(2,1)S(1)}, u32[]{:S(2)}, u32[]{:S(2)}) %all-to-all-start.1) | async-done | bytes 276512 | tf_op jit(solution)/shard_map/all_to_all | solution.py:85
  60.3 1.9 %reshape.92 = bf16[1440,4,24]{2,1,0:T(4,128)(2,1)S(1)} reshape(bf16[16,2,4320]{2,1,0:T(2,128)(2,1)S(1)} %all-to-all-done.1) | data formatting | bytes 552960
  62.1 2.2 %copy.55 = f32[4,16,90,24]{2,3,1,0:T(8,128)S(1)} copy(bf16[4,16,90,24]{3,0,2,1:T(4,128)(2,1)S(1)} %bitcast.187) | data formatting | bytes 829440 | tf_op jit(solution)/shard_map/convert_element_type | solution.py:88
  65.1 2.0 %fusion.35 = bf16[4,90,384]{2,1,0:T(8,128)(2,1)S(1)} fusion(bf16[768,384]{1,0:T(8,128)(2,1)S(1)} %copy-done, bf16[384,768]{1,0:T(8,128)(2,1)} %param.17, f32[4,90]{1,0:T(4,128)S(1)} %add_rsqrt_fusion.1, f32[4,90]{1,0:T(4,128)S(1)} %broadcast_multiply_fusion.1, f32[4,90,384]{2,1,0:T(8,128)S(1)} %copy.56, bf16[4,90,384]{2,0,1:T(4,128)(2,1)S(1)} %copy-done.2), kind=kOutput, calls=%fused_computation.37 | convolution fusion | flops 428405760 | bytes 2288448 | tf_op jit(solution)/shard_map/dot_general | solution.py:93
  67.9 6.4 %collective-permute-start = (bf16[4,90,16]{1,0,2:T(4,128)(2,1)S(1)}, bf16[4,90,16]{1,0,2:T(4,128)(2,1)S(1)}, u32[]{:S(2)}, u32[]{:S(2)}) collective-permute-start(bf16[4,90,16]{1,0,2:T(4,128)(2,1)S(1)} %bitcast.196), channel_id=1, source_target_pairs={{16,0},{32,16},{48,32},{64,48},{80,64},{96,80},{112,96},{128,112},... | collective-permute-start | bytes 34568 | tf_op jit(solution)/shard_map/ppermute | solution.py:16
  77.4 2.9 %collective-permute-done.2 = bf16[4,90,16]{1,0,2:T(4,128)(2,1)S(1)} collective-permute-done((bf16[4,90,16]{1,0,2:T(4,128)(2,1)S(1)}, bf16[4,90,16]{1,0,2:T(4,128)(2,1)S(1)}, u32[]{:S(2)}, u32[]{:S(2)}) %collective-permute-start.2) | collective-permute-done | bytes 11552 | tf_op jit(solution)/shard_map/ppermute | solution.py:16
  81.1 2.5 %collective-permute-start.3 = (bf16[3,90,200]{2,1,0:T(8,128)(2,1)S(1)}, bf16[3,90,200]{2,1,0:T(8,128)(2,1)S(1)}, u32[]{:S(2)}, u32[]{:S(2)}) collective-permute-start(bf16[3,90,200]{2,1,0:T(8,128)(2,1)S(1)} %get-tuple-element.22), channel_id=1, source_target_pairs={{0,16},{16,32},{32,48},{48,64},{64,80},{80,96},{96,112},{112,128},... | collective-permute-start | bytes 324008 | tf_op jit(solution)/shard_map/ppermute | solution.py:26
  83.7 2.1 %collective-permute-done.3 = bf16[3,90,200]{2,1,0:T(8,128)(2,1)S(1)} collective-permute-done((bf16[3,90,200]{2,1,0:T(8,128)(2,1)S(1)}, bf16[3,90,200]{2,1,0:T(8,128)(2,1)S(1)}, u32[]{:S(2)}, u32[]{:S(2)}) %collective-permute-start.3) | collective-permute-done | bytes 108032 | tf_op jit(solution)/shard_map/ppermute | solution.py:26
  85.8 2.5 %collective-permute-done.4 = bf16[3,90,200]{2,1,0:T(8,128)(2,1)S(1)} collective-permute-done((bf16[3,90,200]{2,1,0:T(8,128)(2,1)S(1)}, bf16[3,90,200]{2,1,0:T(8,128)(2,1)S(1)}, u32[]{:S(2)}, u32[]{:S(2)}) %collective-permute-start.4) | collective-permute-done | bytes 108032 | tf_op jit(solution)/shard_map/ppermute | solution.py:27
  88.3 2.2 %collective-permute-start.5 = (bf16[12,3,200]{2,1,0:T(4,128)(2,1)S(1)}, bf16[12,3,200]{2,1,0:T(4,128)(2,1)S(1)}, u32[]{:S(2)}, u32[]{:S(2)}) collective-permute-start(bf16[12,3,200]{2,1,0:T(4,128)(2,1)S(1)} %get-tuple-element.16), channel_id=1, source_target_pairs={{0,1},{1,2},{2,3},{3,4},{4,5},{5,6},{6,7},{7,8},{8,9},{9,10},{10,1... | collective-permute-start | bytes 43208 | tf_op jit(solution)/shard_map/ppermute | solution.py:26
  90.5 6.4 %collective-permute-start.6 = (bf16[12,3,200]{2,1,0:T(4,128)(2,1)S(1)}, bf16[12,3,200]{2,1,0:T(4,128)(2,1)S(1)}, u32[]{:S(2)}, u32[]{:S(2)}) collective-permute-start(bf16[12,3,200]{2,1,0:T(4,128)(2,1)S(1)} %get-tuple-element.17), channel_id=1, source_target_pairs={{1,0},{2,1},{3,2},{4,3},{5,4},{6,5},{7,6},{8,7},{9,8},{10,9},{11,1... | collective-permute-start | bytes 43208 | tf_op jit(solution)/shard_map/ppermute | solution.py:27
  98.1 4.3 %fusion.168 = (f32[6,90]{1,0:T(8,128)S(1)}, f32[6,90,200]{2,1,0:T(8,128)S(1)}) fusion(f32[12,96,200]{2,1,0:T(8,128)S(1)} %fusion.103, f32[200]{0:T(256)S(1)} %bitcast.244, f32[200]{0:T(256)S(1)} %bitcast.245, f32[200]{0:T(256)S(1)} %bitcast.198, f32[200]{0:T(256)S(1)} %bitcast.199, f32[200]{0:T(256)S(1)} %bitcast.200, f32[200]{0:T(256)S(1)} %bitcast.201, ...), kind=kLoop, calls=%fused_computation.255 | loop fusion | flops 10583460 | bytes 21641360 | tf_op jit(solution)/shard_map/reduce_sum | solution.py:33
  104.7 3.0 %collective-permute-start.7 = (bf16[4,90,16]{1,0,2:T(4,128)(2,1)S(1)}, bf16[4,90,16]{1,0,2:T(4,128)(2,1)S(1)}, u32[]{:S(2)}, u32[]{:S(2)}) collective-permute-start(bf16[4,90,16]{1,0,2:T(4,128)(2,1)S(1)} %convolution_convert_fusion.4), channel_id=1, source_target_pairs={{0,16},{16,32},{32,48},{48,64},{64,80},{80,96},{96,112},{112,128},... | collective-permute-start | bytes 34568 | tf_op jit(solution)/shard_map/ppermute | solution.py:16
  107.8 3.6 %collective-permute-start.8 = (bf16[4,90,16]{1,0,2:T(4,128)(2,1)S(1)}, bf16[4,90,16]{1,0,2:T(4,128)(2,1)S(1)}, u32[]{:S(2)}, u32[]{:S(2)}) collective-permute-start(bf16[4,90,16]{1,0,2:T(4,128)(2,1)S(1)} %convolution_convert_fusion.3), channel_id=1, source_target_pairs={{0,32},{16,48},{32,64},{48,80},{64,96},{80,112},{96,128},{112,144}... | collective-permute-start | bytes 34568 | tf_op jit(solution)/shard_map/ppermute | solution.py:16
  111.4 5.3 %collective-permute-start.9 = (bf16[4,90,16]{1,0,2:T(4,128)(2,1)S(1)}, bf16[4,90,16]{1,0,2:T(4,128)(2,1)S(1)}, u32[]{:S(2)}, u32[]{:S(2)}) collective-permute-start(bf16[4,90,16]{1,0,2:T(4,128)(2,1)S(1)} %convolution_convert_fusion.2), channel_id=1, source_target_pairs={{0,48},{16,64},{32,80},{48,96},{64,112},{80,128},{96,144},{112,160... | collective-permute-start | bytes 34568 | tf_op jit(solution)/shard_map/ppermute | solution.py:16
  (102 shorter events, 13.2 us)
Async XLA Ops:
  0.6 64.5 %copy-start = (bf16[768,384]{1,0:T(8,128)(2,1)S(1)}, bf16[768,384]{1,0:T(8,128)(2,1)}, u32[]{:S(2)}) copy-start(bf16[768,384]{1,0:T(8,128)(2,1)} %param.18) | copy-start | bytes 1769476
  2.7 27.6 %all-to-all-start = ((bf16[4,90,384]{1,0,2:T(4,128)(2,1)}), bf16[4,90,384]{1,0,2:T(4,128)(2,1)S(1)}, u32[]{:S(2)}, u32[]{:S(2)}) async-start(bf16[4,90,384]{1,0,2:T(4,128)(2,1)} %copy.51), calls=%async_computation | async-start | bytes 786432 | tf_op jit(solution)/shard_map/all_to_all | solution.py:74
  10.3 19.6 %copy-start.12 = (s32[32,1,4]{0,2,1:T(4,128)S(1)}, s32[32,1,4]{0,2,1:T(4,128)}, u32[]{:S(2)}) copy-start(s32[32,1,4]{0,2,1:T(4,128)} %param.20) | copy-start | bytes 1540
  10.3 19.7 %copy-start.13 = (s32[32,1]{0,1:T(1,128)S(1)}, s32[32,1]{0,1:T(1,128)}, u32[]{:S(2)}) copy-start(s32[32,1]{0,1:T(1,128)} %param.21) | copy-start | bytes 388
  10.3 19.8 %copy-start.7 = (f32[7,7,200]{2,1,0:T(8,128)S(1)}, f32[7,7,200]{2,1,0:T(8,128)}, u32[]{:S(2)}) copy-start(f32[7,7,200]{2,1,0:T(8,128)} %param.25) | copy-start | bytes 117604
  10.3 20.0 %copy-start.6 = (f32[2,720,24]{1,2,0:T(8,128)S(1)}, f32[2,720,24]{1,2,0:T(8,128)}, u32[]{:S(2)}) copy-start(f32[2,720,24]{1,2,0:T(8,128)} %param.16) | copy-start | bytes 414724
  30.8 6.1 %slice-start.1 = ((s8[4423680]{0:T(1024)(128)(4,1)}), s8[4194304]{0:T(1024)(128)(4,1)S(1)}, s32[]{:S(2)}) async-start(s8[4423680]{0:T(1024)(128)(4,1)} %bitcast.184), calls=%async_computation.3 | async-start | bytes 8388608
  38.7 13.9 %copy-start.5 = (f32[6,32,4]{1,2,0:T(4,128)S(1)}, f32[6,32,4]{1,2,0:T(4,128)}, u32[]{:S(2)}) copy-start(f32[6,32,4]{1,2,0:T(4,128)} %param.22) | copy-start | bytes 9220
  41.7 23.0 %copy-start.2 = (bf16[4,90,384]{2,0,1:T(4,128)(2,1)S(1)}, bf16[4,90,384]{2,0,1:T(4,128)(2,1)}, u32[]{:S(2)}) copy-start(bf16[4,90,384]{2,0,1:T(4,128)(2,1)} %param.15) | copy-start | bytes 829444
  46.0 14.3 %all-to-all-start.1 = ((bf16[16,2,4320]{2,1,0:T(2,128)(2,1)}), bf16[16,2,4320]{2,1,0:T(2,128)(2,1)S(1)}, u32[]{:S(2)}, u32[]{:S(2)}) async-start(bf16[16,2,4320]{2,1,0:T(2,128)(2,1)} %reshape.91), calls=%async_computation.1 | async-start | bytes 557056 | tf_op jit(solution)/shard_map/all_to_all | solution.py:85
  64.8 16.0 %copy-start.4 = (bf16[6,90,200]{2,1,0:T(8,128)(2,1)S(1)}, bf16[6,90,200]{2,1,0:T(8,128)(2,1)}, u32[]{:S(2)}) copy-start(bf16[6,90,200]{2,1,0:T(8,128)(2,1)} %param.23) | copy-start | bytes 648004
  64.8 16.0 %copy-start.9 = (bf16[16,200]{1,0:T(8,128)(2,1)S(1)}, bf16[16,200]{1,0:T(8,128)(2,1)}, u32[]{:S(2)}) copy-start(bf16[16,200]{1,0:T(8,128)(2,1)} %param.24) | copy-start | bytes 19204
  65.1 31.8 %copy-start.11 = (s32[6,90]{1,0:T(8,128)S(1)}, s32[6,90]{1,0:T(8,128)}, u32[]{:S(2)}) copy-start(s32[6,90]{1,0:T(8,128)} %param.29) | copy-start | bytes 6484
  67.9 9.3 %collective-permute-start = (bf16[4,90,16]{1,0,2:T(4,128)(2,1)S(1)}, bf16[4,90,16]{1,0,2:T(4,128)(2,1)S(1)}, u32[]{:S(2)}, u32[]{:S(2)}) collective-permute-start(bf16[4,90,16]{1,0,2:T(4,128)(2,1)S(1)} %bitcast.196), channel_id=1, source_target_pairs={{16,0},{32,16},{48,32},{64,48},{80,64},{96,80},{112,96},{128,112},... | collective-permute-start | bytes 34568 | tf_op jit(solution)/shard_map/ppermute | solution.py:16
  74.3 6.0 %collective-permute-start.2 = (bf16[4,90,16]{1,0,2:T(4,128)(2,1)S(1)}, bf16[4,90,16]{1,0,2:T(4,128)(2,1)S(1)}, u32[]{:S(2)}, u32[]{:S(2)}) collective-permute-start(bf16[4,90,16]{1,0,2:T(4,128)(2,1)S(1)} %bitcast.194), channel_id=1, source_target_pairs={{48,0},{64,16},{80,32},{96,48},{112,64},{128,80},{144,96},{160,112... | collective-permute-start | bytes 34568 | tf_op jit(solution)/shard_map/ppermute | solution.py:16
  75.6 4.9 %collective-permute-start.1 = (bf16[4,90,16]{1,0,2:T(4,128)(2,1)S(1)}, bf16[4,90,16]{1,0,2:T(4,128)(2,1)S(1)}, u32[]{:S(2)}, u32[]{:S(2)}) collective-permute-start(bf16[4,90,16]{1,0,2:T(4,128)(2,1)S(1)} %bitcast.195), channel_id=1, source_target_pairs={{32,0},{48,16},{64,32},{80,48},{96,64},{112,80},{128,96},{144,112}... | collective-permute-start | bytes 34568 | tf_op jit(solution)/shard_map/ppermute | solution.py:16
  81.1 4.6 %collective-permute-start.3 = (bf16[3,90,200]{2,1,0:T(8,128)(2,1)S(1)}, bf16[3,90,200]{2,1,0:T(8,128)(2,1)S(1)}, u32[]{:S(2)}, u32[]{:S(2)}) collective-permute-start(bf16[3,90,200]{2,1,0:T(8,128)(2,1)S(1)} %get-tuple-element.22), channel_id=1, source_target_pairs={{0,16},{16,32},{32,48},{48,64},{64,80},{80,96},{96,112},{112,128},... | collective-permute-start | bytes 324008 | tf_op jit(solution)/shard_map/ppermute | solution.py:26
  83.7 4.6 %collective-permute-start.4 = (bf16[3,90,200]{2,1,0:T(8,128)(2,1)S(1)}, bf16[3,90,200]{2,1,0:T(8,128)(2,1)S(1)}, u32[]{:S(2)}, u32[]{:S(2)}) collective-permute-start(bf16[3,90,200]{2,1,0:T(8,128)(2,1)S(1)} %get-tuple-element.23), channel_id=1, source_target_pairs={{16,0},{32,16},{48,32},{64,48},{80,64},{96,80},{112,96},{128,112},... | collective-permute-start | bytes 324008 | tf_op jit(solution)/shard_map/ppermute | solution.py:27
  88.3 9.5 %collective-permute-start.5 = (bf16[12,3,200]{2,1,0:T(4,128)(2,1)S(1)}, bf16[12,3,200]{2,1,0:T(4,128)(2,1)S(1)}, u32[]{:S(2)}, u32[]{:S(2)}) collective-permute-start(bf16[12,3,200]{2,1,0:T(4,128)(2,1)S(1)} %get-tuple-element.16), channel_id=1, source_target_pairs={{0,1},{1,2},{2,3},{3,4},{4,5},{5,6},{6,7},{7,8},{8,9},{9,10},{10,1... | collective-permute-start | bytes 43208 | tf_op jit(solution)/shard_map/ppermute | solution.py:26
  90.5 7.4 %collective-permute-start.6 = (bf16[12,3,200]{2,1,0:T(4,128)(2,1)S(1)}, bf16[12,3,200]{2,1,0:T(4,128)(2,1)S(1)}, u32[]{:S(2)}, u32[]{:S(2)}) collective-permute-start(bf16[12,3,200]{2,1,0:T(4,128)(2,1)S(1)} %get-tuple-element.17), channel_id=1, source_target_pairs={{1,0},{2,1},{3,2},{4,3},{5,4},{6,5},{7,6},{8,7},{9,8},{10,9},{11,1... | collective-permute-start | bytes 43208 | tf_op jit(solution)/shard_map/ppermute | solution.py:27
  103.8 14.8 %copy-start.3 = (bf16[6,90,200]{2,1,0:T(8,128)(2,1)}, bf16[6,90,200]{2,1,0:T(8,128)(2,1)S(1)}, u32[]{:S(2)}) copy-start(bf16[6,90,200]{2,1,0:T(8,128)(2,1)S(1)} %fusion.33) | copy-start | bytes 648004
  104.7 12.2 %collective-permute-start.7 = (bf16[4,90,16]{1,0,2:T(4,128)(2,1)S(1)}, bf16[4,90,16]{1,0,2:T(4,128)(2,1)S(1)}, u32[]{:S(2)}, u32[]{:S(2)}) collective-permute-start(bf16[4,90,16]{1,0,2:T(4,128)(2,1)S(1)} %convolution_convert_fusion.4), channel_id=1, source_target_pairs={{0,16},{16,32},{32,48},{48,64},{64,80},{80,96},{96,112},{112,128},... | collective-permute-start | bytes 34568 | tf_op jit(solution)/shard_map/ppermute | solution.py:16
  107.8 10.0 %collective-permute-start.8 = (bf16[4,90,16]{1,0,2:T(4,128)(2,1)S(1)}, bf16[4,90,16]{1,0,2:T(4,128)(2,1)S(1)}, u32[]{:S(2)}, u32[]{:S(2)}) collective-permute-start(bf16[4,90,16]{1,0,2:T(4,128)(2,1)S(1)} %convolution_convert_fusion.3), channel_id=1, source_target_pairs={{0,32},{16,48},{32,64},{48,80},{64,96},{80,112},{96,128},{112,144}... | collective-permute-start | bytes 34568 | tf_op jit(solution)/shard_map/ppermute | solution.py:16
  111.4 6.1 %collective-permute-start.9 = (bf16[4,90,16]{1,0,2:T(4,128)(2,1)S(1)}, bf16[4,90,16]{1,0,2:T(4,128)(2,1)S(1)}, u32[]{:S(2)}, u32[]{:S(2)}) collective-permute-start(bf16[4,90,16]{1,0,2:T(4,128)(2,1)S(1)} %convolution_convert_fusion.2), channel_id=1, source_target_pairs={{0,48},{16,64},{32,80},{48,96},{64,112},{80,128},{96,144},{112,160... | collective-permute-start | bytes 34568 | tf_op jit(solution)/shard_map/ppermute | solution.py:16
  (6 other events, 25.4 us)
where the time goes:
time: 119 us
  starting transfers between devices  46.3 us (39%)
  other arithmetic  25.4 us (21%)
  matrix products  16.1 us (14%)
  waiting for transfers between devices  14.9 us (13%)
  local copies, waits for them, and re-layouts  14.5 us (12%)
  between operations  1.36 us (1%)
    ppermute x6, starting transfers between devices, passed_along(): return lax.ppermute(value, axis, pairs)  20.9 us
    sin x1, other arithmetic, wave_table(): return jnp.concatenate([jnp.cos(angle), jnp.sin(angle)], axis=0)  19.6 us
    unnamed x41, local copies, waits for them, and re-layouts  8.95 us
    all_to_all x1, starting transfers between devices, per_device(): lax.all_to_all(atm_state, 'col', split_axis=2, concat_axis=1, tiled=True)  7.58 us
    all_to_all x1, waiting for transfers between devices, per_device(): lax.all_to_all(zonal.astype(jnp.bfloat16), 'col', split_axis=1, concat_ax...  6.92 us
    unnamed x2, matrix products  6.69 us
    all_to_all x1, starting transfers between devices, per_device(): lax.all_to_all(zonal.astype(jnp.bfloat16), 'col', split_axis=1, concat_ax...  6.67 us
    ppermute x2, starting transfers between devices, with_halo(): after = lax.ppermute(initial, axis, down)  6.42 us
  transfers between devices with their start and end apart: 12, of which 5 were waited for; matrix products, arithmetic and copies ran while one was open for 19% of the time, Pallas kernels for 0%

commit v1 on v0

v1 whole, which is shorter than its diff:
```python
import functools

import jax
import jax.numpy as jnp
import numpy as np
from jax import lax
from jax.experimental import pallas as pl
from jax.experimental.pallas import tpu as pltpu
from jax.sharding import PartitionSpec as P

F32 = jnp.float32
BF16 = jnp.bfloat16
MESH = pl.DeviceIdType.MESH
ANY = pl.ANY

SPAN = 4
LATS = 4
SLOTS = 4
LON = 1440
WAVES = 720
LOCAL = 90
PAD = 96
RIM = 3
KS = 7
CH = 384
OWN = 24
HALF = LON // 2
BLOCKS = 8
TAB = BLOCKS * PAD
WPAD = TAB // 2
ROWS = 6
HO = 200
HP = 256
FIELDS = 16
NT = (((1,), (1,)), ((), ()))


def tables():
    place = np.arange(PAD)
    block = np.arange(BLOCKS)
    inside = np.broadcast_to(place < LOCAL, (BLOCKS, PAD)).reshape(-1)
    lon_in = (LOCAL * block[:, None] + place[None]).reshape(-1)
    rim = np.where(place < LOCAL + RIM, place, place - PAD)
    lon_out = (LOCAL * block[:, None] + rim[None]).reshape(-1)
    forward = np.zeros((2, TAB, TAB), np.float64)
    inverse = np.zeros((2, TAB, TAB), np.float64)
    deal = np.zeros((2 * WPAD, TAB), np.float64)
    count = WAVES // 2
    for parity in range(2):
        wave = 2 * np.arange(count) + parity
        angle = 2 * np.pi * (wave[:, None] * lon_in[None] % LON) / LON
        forward[parity, :count] = np.cos(angle) * inside
        forward[parity, WPAD : WPAD + count] = np.sin(angle) * inside
        angle = 2 * np.pi * (lon_out[:, None] * wave[None] % LON) / LON
        inverse[parity, :, :count] = np.cos(angle)
        inverse[parity, :, WPAD : WPAD + count] = np.sin(angle)
        deal[parity * WPAD + np.arange(count), wave] = 1.0
    return [t.astype(np.float32).astype(jnp.bfloat16) for t in (forward, inverse, deal)]


def iota(shape, axis):
    return lax.broadcasted_iota(jnp.int32, shape, axis)


def one_hot(condition):
    return jnp.where(condition, 1.0, 0.0).astype(BF16)


def dot(a, b):
    return jnp.dot(a, b, preferred_element_type=F32)


def dot_nt(a, b):
    return lax.dot_general(a, b, NT, preferred_element_type=F32)


def windows(tile):
    out = []
    for d in range(16):
        lo, hi = max(OWN * d, 128 * tile), min(OWN * d + OWN, 128 * tile + 128)
        if lo < hi:
            out.append((d, lo, hi - lo))
    return out


def body(
    bands,
    cols,
    atm,
    gain,
    w_in,
    w_out,
    flux_t,
    p_rows,
    p_count,
    p_weight,
    ocean,
    force,
    kernel_w,
    o_in,
    o_out_t,
    surf_t,
    land,
    tab_f,
    tab_i,
    deal,
    atm_out,
    ocean_out,
    surf_out,
    xv,
    st,
    x32,
    rolled,
    send1,
    recv1,
    send2,
    recv2,
    tf,
    ti,
    dl,
    gv,
    gx,
    gt,
    w1,
    w2,
    fpt,
    ocv,
    oc,
    obs,
    obr,
    ohs,
    ohr,
    ahs,
    ahr,
    sel,
    selr,
    wown,
    wr,
    kv,
    kp,
    fp,
    fpc,
    oin,
    oot,
    spt,
    lm,
    lmp,
    s0,
    biga,
    bigb,
    wst,
    xs,
    fxt,
    sxt,
    mx,
    nx,
    flx,
    flr,
    bks,
    bkr,
    ao,
    oo,
    so,
    ld,
    out_sem,
    a1s,
    a1r,
    a2s,
    a2r,
    sls,
    slr,
    ws,
    wrs,
    ohss,
    ohrs,
    obss,
    obrs,
    ahss,
    ahrs,
    fls,
    flrs,
    bss,
    brs,
):
    me = lax.axis_index("col")
    band = lax.axis_index("band")

    def col_at(k):
        return lax.rem(me + k + cols, cols)

    def band_at(k):
        return lax.rem(band + k + bands, bands)

    def load(src, dst, k):
        c = pltpu.make_async_copy(src, dst, ld.at[k])
        c.start()
        return c

    l_atm = load(atm, xv, 0)
    l_ocean = load(ocean, ocv, 1)
    l_force = load(force, fp, 2)
    l_kernel = load(kernel_w, kv, 3)
    l_gain = load(gain, gv, 4)
    l_deal = load(deal, dl, 5)
    l_tf = load(tab_f, tf, 6)
    l_flux = load(flux_t, fpt, 7)
    l_surf = load(surf_t, spt, 8)
    l_land = load(land, lm, 9)
    l_ti = load(tab_i, ti, 10)
    l_w1 = load(w_in, w1, 11)
    l_w2 = load(w_out, w2, 12)
    l_oin = load(o_in, oin, 13)
    l_oot = load(o_out_t, oot, 14)

    barrier = pltpu.get_barrier_semaphore()
    for k in range(1, cols):
        pl.semaphore_signal(barrier, inc=1, device_id={"col": col_at(k)}, device_id_type=MESH)
    for k in (1, 2, 3, 4):
        for sign in (1, -1):
            pl.semaphore_signal(
                barrier, inc=1, device_id={"band": band_at(sign * k)}, device_id_type=MESH
            )

    def remote(src, dst, send_sem, recv_sem, device):
        return pltpu.make_async_remote_copy(
            src_ref=src,
            dst_ref=dst,
            send_sem=send_sem,
            recv_sem=recv_sem,
            device_id=device,
            device_id_type=MESH,
        )

    lane = iota((PAD, 128), 1)
    st[:, LATS * LOCAL :, :] = jnp.zeros((3, LATS * (PAD - LOCAL), 128), F32)
    l_atm.wait()
    for l in range(LOCAL):
        for t in range(3):
            cut = slice(128 * t, 128 * t + 128)
            st[t, LATS * l : LATS * l + LATS, :] = xv[l, :, cut].astype(F32)
    for a in range(LATS):
        for t in range(3):
            part = st.at[t][pl.ds(a, PAD, stride=LATS), :]
            x32[a, :, 128 * t : 128 * t + 128] = part
            rolled[a, t] = pltpu.roll(part, OWN * a, 1) if a else part
    for d in range(cols):
        out = jnp.zeros((PAD, 128), F32)
        for t in range(3):
            for e, lo, n in windows(t):
                if e == d:
                    for a in range(LATS):
                        mask = ((lane - (lo + OWN * a)) & 127) < n
                        out = jnp.where(mask, rolled[a, t], out)
        send1[d] = out.astype(BF16)
    recv1[me] = send1[me]

    row8 = iota((8, 128), 0)
    lane8 = iota((8, 128), 1)
    zero8 = jnp.zeros((8, 128), F32)
    for q in (0, 1, 6, 7):
        sel[q] = zero8
    for k in range(SPAN):
        other = band - k
        at = jnp.maximum(other, 0)
        used = jnp.where(other >= 0, p_count[0, at], 0)
        vec = zero8
        for p in range(SLOTS):
            target = jnp.where(p < used, SLOTS * p_rows[0, p, at] + p, -1)
            vec = jnp.where(lane8 == target, 1.0, vec)
        sel[5 - k] = vec
    vec = zero8
    for o in range(SPAN):
        at = jnp.minimum(band + o, bands - 1)
        for p in range(SLOTS):
            here = (lane8 // 16 == o) & (lane8 % SLOTS == p)
            for i in range(ROWS):
                vec = jnp.where(here & (row8 == i), p_weight[i, p, at], vec)
    wown[...] = vec

    pl.semaphore_wait(barrier, cols - 1 + 8)

    a1 = []
    for k in range(1, cols):
        d = col_at(k)
        c = remote(send1.at[d], recv1.at[me], a1s.at[k], a1r.at[k], {"col": d})
        c.start()
        a1.append(c)

    l_ocean.wait()
    oc[RIM : RIM + ROWS] = jnp.zeros((ROWS, PAD, HP), F32)
    oc[RIM : RIM + ROWS, 0:LOCAL, 0:HO] = ocv[...].astype(F32)
    for i in range(ROWS):
        ohs[0, i] = pltpu.roll(oc[RIM + i, 0:8, :], 2, 0)
        ohs[1, i] = pltpu.roll(oc[RIM + i, 80:96, :], 6, 0)[8:16]
    oh = []
    for side, k in ((0, -1), (1, 1)):
        c = remote(ohs.at[side], ohr.at[side], ohss.at[side], ohrs.at[side], {"col": col_at(k)})
        c.start()
        oh.append(c)
    small = []
    for o in (0, 2, 3, 4, 5):
        c = remote(
            sel.at[pl.ds(5 - o, 3)], selr.at[o], sls.at[o], slr.at[o], {"band": band_at(1 - o)}
        )
        c.start()
        small.append(c)
    for side, k in ((0, 1), (1, -1)):
        c = remote(wown, wr.at[side], ws.at[side], wrs.at[side], {"band": band_at(k)})
        c.start()
        small.append(c)
    selr[1] = sel[4:7]

    for a in range(LATS):
        ahs[0, a] = pltpu.roll(x32[a, 0:8, :], 2, 0)
        ahs[1, a] = pltpu.roll(x32[a, 80:96, :], 6, 0)[8:16]

    l_gain.wait()
    gx[...] = jnp.zeros(gx.shape, F32)
    for a in range(LATS):
        for q in range(OWN // 8):
            row = pl.multiple_of(lax.rem(OWN * (me + a) + 8 * q, 128), 8)
            gx[:, pl.ds(row, 8), 0:WAVES] = gv[:, 8 * q : 8 * q + 8, :] * (2.0 / LON)
    l_deal.wait()
    for part in range(2):
        g = gx[part]
        high = g.astype(BF16)
        low = (g - high.astype(F32)).astype(BF16)
        both = dot_nt(dl[...], jnp.concatenate([high, low], axis=0))
        gt[part] = both[:, :128] + both[:, 128:]

    l_force.wait()
    l_kernel.wait()
    kp[...] = jnp.zeros(kp.shape, F32)
    kp[:, 0:KS, 0:HO] = kv[...]
    f32_force = fp[...].astype(F32)
    wst[...] = jnp.zeros(wst.shape, BF16)
    fpc[...] = jnp.zeros(fpc.shape, BF16)
    for dj in range(KS):
        for di in range(KS):
            at = 128 * dj + FIELDS * di
            wst[at : at + FIELDS, 0:HO] = (f32_force * kp[di, dj : dj + 1, 0:HO]).astype(BF16)
    fpc[FIELDS * RIM : FIELDS * RIM + FIELDS, 0:HO] = fp[...]

    l_flux.wait()
    r, f = iota((512, FIELDS), 0), iota((512, FIELDS), 1)
    spread = one_hot((r % 64 // 16 == r // 128) & (r % 16 == f))
    fxt[...] = dot(spread, fpt[...]).astype(BF16)
    l_surf.wait()
    r, f = iota((768, FIELDS), 0), iota((768, FIELDS), 1)
    spread = one_hot((r % 128 // 16 == r // 128) & (r % 16 == f))
    sxt[...] = dot(spread, spt[...]).astype(BF16)
    l_land.wait()
    lmp[...] = jnp.zeros(lmp.shape, F32)
    lmp[0:ROWS, 0:LOCAL] = lm[...].astype(F32)

    for c in oh:
        c.wait()
    sub = iota((8, HP), 0)
    for i in range(ROWS):
        tile = oc[RIM + i, 88:96, :]
        oc[RIM + i, 88:96, :] = jnp.where(
            sub < 2, tile, jnp.where(sub < 5, ohr[0, i], ohr[1, i])
        )
    obs[...] = oc[RIM : RIM + ROWS].astype(BF16)
    ob = []
    for side, k in ((1, -1), (0, 1)):
        src = obs.at[pl.ds(RIM * (1 - side), RIM)]
        c = remote(src, obr.at[side], obss.at[side], obrs.at[side], {"band": band_at(k)})
        c.start()
        ob.append(c)

    for c in small:
        c.wait()
    up_ok = jnp.where(band > 0, 1.0, 0.0).astype(F32)
    down_ok = jnp.where(band < bands - 1, 1.0, 0.0).astype(F32)
    blocks = []
    for b in range(3):
        chosen = selr[0, b]
        for o in range(1, 6):
            chosen = chosen + pltpu.roll(selr[o, b], 16 * o, 1)
        if b == 0:
            blocks.append(wr[0] * chosen * up_ok)
        elif b == 1:
            blocks.append(pltpu.roll(wown[...], 16, 1) * chosen)
        else:
            blocks.append(pltpu.roll(wr[1], 32, 1) * chosen * down_ok)
    slots = jnp.concatenate(blocks, axis=0).astype(BF16)
    r, c_ = iota((384, 128), 0), iota((384, 128), 1)
    by_row = dot_nt(one_hot(r // 16 == c_ // 4), slots).astype(BF16)
    r, c_ = iota((24, 768), 0), iota((24, 768), 1)
    tap = c_ % 128 // 16
    need = c_ // 128 + tap
    has = r % 8 + jnp.where(r < 8, -RIM, jnp.where(r < 16, RIM, RIM + ROWS))
    legal = (
        (tap < KS)
        & ((r >= 8) | (r % 8 >= ROWS - RIM))
        & (r % 8 < ROWS)
        & ((r < 16) | (r % 8 < RIM))
    )
    spread = one_hot(legal & (need == has))
    r, c_ = iota((384, 768), 0), iota((384, 768), 1)
    biga[...] = jnp.where(r % 16 == c_ % 16, dot(by_row, spread), 0.0).astype(BF16)
    r, c_ = iota((128, 24), 0), iota((128, 24), 1)
    by_own = dot(one_hot((c_ - 8 == r // 16) & (r // 16 < ROWS)), slots).astype(BF16)
    r, c_ = iota((256, 128), 0), iota((256, 128), 1)
    full = dot_nt(one_hot(c_ // 4 == 4 * (r // 64 + 1) + r % 64 // 16), by_own)
    bigb[...] = jnp.where(r % 16 == c_ % 16, full, 0.0).astype(BF16)

    l_tf.wait()
    for c in a1:
        c.wait_recv()
    ah = []
    for side, k in ((0, -1), (1, 1)):
        c = remote(ahs.at[side], ahr.at[side], ahss.at[side], ahrs.at[side], {"col": col_at(k)})
        c.start()
        ah.append(c)
    first = recv1[0:BLOCKS].reshape(TAB, 128).astype(F32)
    second = recv1[BLOCKS : 2 * BLOCKS].reshape(TAB, 128).astype(F32)
    waves = []
    for parity in range(2):
        mix = first - second if parity else first + second
        spec = dot(tf[parity], mix.astype(BF16))
        real, imag = spec[:WPAD], spec[WPAD:]
        rows = slice(parity * WPAD, parity * WPAD + WPAD)
        g_real, g_imag = gt[0, rows], gt[1, rows]
        waves.append(
            jnp.concatenate(
                [g_real * real + g_imag * imag, g_real * imag - g_imag * real], axis=0
            ).astype(BF16)
        )
    l_ti.wait()
    chunk = 2
    parts = BLOCKS // chunk
    for k in range(parts):
        q = lax.rem(me // chunk + k, parts)
        rows = pl.ds(pl.multiple_of(q * (chunk * PAD), chunk * PAD), chunk * PAD)
        even = dot(ti[0, rows, :], waves[0])
        odd = dot(ti[1, rows, :], waves[1])
        send2[pl.ds(q * chunk, chunk)] = (even + odd).astype(BF16).reshape(chunk, PAD, 128)
        send2[pl.ds(q * chunk + BLOCKS, chunk)] = (
            (even - odd).astype(BF16).reshape(chunk, PAD, 128)
        )
        for n in range(2 * chunk):
            to = q * chunk + n % chunk + BLOCKS * (n // chunk)
            step = lax.rem(to - me + cols, cols)

            @pl.when(to != me)
            def _():
                remote(
                    send2.at[to], recv2.at[me], a2s.at[step], a2r.at[step], {"col": to}
                ).start()

    recv2[me] = send2[me]

    for c in ob:
        c.wait()
    oc[0:RIM] = obr[0].astype(F32) * up_ok
    oc[RIM + ROWS :] = obr[1].astype(F32) * down_ok

    def stencil_row(i, carry):
        for t in range(HP // 128):
            cut = slice(128 * t, 128 * t + 128)
            total = None
            for dj in range(KS):
                line = None
                for di in range(KS):
                    term = kp[di, dj : dj + 1, cut] * oc[i + di, :, cut]
                    line = term if line is None else line + term
                shift = (RIM - dj) % PAD
                line = pltpu.roll(line, shift, 0) if shift else line
                total = line if total is None else total + line
            s0[i, :, cut] = total
        return carry

    lax.fori_loop(0, ROWS, stencil_row, 0)

    for c in ah:
        c.wait()
    sub = iota((8, CH), 0)
    for a in range(LATS):
        tile = x32[a, 88:96, :]
        x32[a, 88:96, :] = jnp.where(sub < 2, tile, jnp.where(sub < 5, ahr[0, a], ahr[1, a]))
    for k in range(1, cols):
        remote(send2.at[0], recv2.at[0], a2s.at[k], a2r.at[k], {"col": col_at(k)}).wait_recv()
    for a in range(LATS):
        for t in range(3):
            cut = slice(128 * t, 128 * t + 128)
            zonal = jnp.zeros((PAD, 128), F32)
            for d, lo, n in windows(t):
                mask = ((lane - (lo + OWN * a)) & 127) < n
                zonal = jnp.where(mask, recv2[d].astype(F32), zonal)
            if a:
                zonal = pltpu.roll(zonal, 128 - OWN * a, 1)
            mx[a * PAD : a * PAD + PAD, cut] = x32[a, :, cut] + zonal
    mixed = mx[...]
    centred = mixed - jnp.mean(mixed, axis=-1, keepdims=True)
    spread = jnp.mean(centred * centred, axis=-1, keepdims=True)
    normed = (centred * lax.rsqrt(spread + 1e-05)).astype(BF16)
    l_w1.wait()
    l_w2.wait()
    inner = jax.nn.gelu(dot(normed, w1[...])).astype(BF16)
    nx[...] = (mx[...] + dot(inner, w2[...])).astype(BF16)
    flux = None
    for a in range(LATS):
        term = dot_nt(nx[a * PAD : a * PAD + PAD, :], fxt[128 * a : 128 * a + 128, :])
        flux = term if flux is None else flux + term
    flx[...] = flux.astype(BF16)
    fl = []
    for o in (0, 2, 3, 4, 5):
        c = remote(flx, flr.at[o], fls.at[o], flrs.at[o], {"band": band_at(1 - o)})
        c.start()
        fl.append(c)
    flr[1] = flx[...]

    for t in range(3):
        cut = slice(128 * t, 128 * t + 128)
        for a in range(LATS):
            part = nx[a * PAD : a * PAD + PAD, cut].astype(F32)
            st.at[t][pl.ds(a, PAD, stride=LATS), :] = part
        for l in range(LOCAL):
            ao[l, :, cut] = st[t, LATS * l : LATS * l + LATS, :].astype(BF16)
    o_atm = pltpu.make_async_copy(ao, atm_out, out_sem.at[0])
    o_atm.start()

    r, c_ = iota((128, 128), 0), iota((128, 128), 1)
    sea = dot_nt(one_hot(r == c_), lmp[...].astype(BF16))
    l_oin.wait()
    l_oot.wait()
    for c in fl:
        c.wait()
    low = iota((PAD, 128), 1) < 64
    tiles = [
        jnp.where(low, flr[2 * q].astype(F32), flr[2 * q + 1].astype(F32)).astype(BF16)
        for q in range(3)
    ]
    forcing = dot(jnp.concatenate(tiles, axis=1), biga[...])
    for i in range(ROWS):
        part = forcing[:, 128 * i : 128 * i + 128]
        for dj in range(KS):
            shift = (RIM - dj) % PAD
            turned = pltpu.roll(part, shift, 0) if shift else part
            xs[PAD * i : PAD * i + PAD, 128 * dj : 128 * dj + 128] = turned.astype(BF16)
    rows = ROWS * PAD
    stencil = (dot(xs[...], wst[...]) + s0[...].reshape(rows, HP))[:, :HO]
    centred = stencil - jnp.mean(stencil, axis=-1, keepdims=True)
    spread = jnp.mean(centred * centred, axis=-1, keepdims=True)
    onorm = (centred * lax.rsqrt(spread + 1e-05)).astype(BF16)
    hidden = jax.nn.gelu(dot(onorm, oin[...])).astype(BF16)
    change = dot_nt(hidden, oot[...])
    pushed = dot(xs[:, 128 * RIM : 128 * RIM + 128], fpc[...])
    lifted = (oc[RIM : RIM + ROWS].reshape(rows, HP) + pushed)[:, :HO].astype(BF16).astype(F32)
    result = lifted + change
    surface = None
    for i in range(ROWS):
        part = (result[PAD * i : PAD * i + PAD] * sea[0:PAD, i : i + 1]).astype(BF16)
        oo[i] = part[:LOCAL]
        term = dot_nt(part, sxt[128 * i : 128 * i + 128, :])
        surface = term if surface is None else surface + term
    back = dot_nt(bigb[...], surface.astype(BF16)).astype(BF16)
    for o in range(SPAN):
        bks[o] = back[64 * o : 64 * o + 64]
    bk = []
    for o in range(1, SPAN):
        c = remote(bks.at[o], bkr.at[o], bss.at[o], brs.at[o], {"band": band_at(o)})
        c.start()
        bk.append(c)
    o_ocean = pltpu.make_async_copy(oo, ocean_out, out_sem.at[1])
    o_ocean.start()
    total = bks[0].astype(F32)
    for c in bk:
        c.wait()
    for o in range(1, SPAN):
        total = total + bkr[o].astype(F32)
    so[...] = total.reshape(LATS, FIELDS, PAD)[:, :, :LOCAL].astype(BF16)
    o_surf = pltpu.make_async_copy(so, surf_out, out_sem.at[2])
    o_surf.start()
    for c in a1:
        c.wait_send()
    for k in range(1, cols):
        remote(send2.at[0], recv2.at[0], a2s.at[k], a2r.at[k], {"col": col_at(k)}).wait_send()
    o_atm.wait()
    o_ocean.wait()
    o_surf.wait()


def per_device(
    bands,
    cols,
    consts,
    atm_state,
    spec_gain,
    mlp_in,
    mlp_out,
    flux_proj,
    pair_rows,
    pair_count,
    pair_weight,
    ocean_state,
    force_proj,
    depth_kernel,
    ocean_in,
    ocean_out,
    surf_proj,
    land_mask,
):
    any_spec = pl.BlockSpec(memory_space=ANY)
    smem = pl.BlockSpec(memory_space=pltpu.SMEM)
    vm = pltpu.VMEM
    dma = pltpu.SemaphoreType.DMA
    scratch = [
        vm((LOCAL, LATS, CH), BF16),
        vm((3, LATS * PAD, 128), F32),
        vm((LATS, PAD, CH), F32),
        vm((LATS, 3, PAD, 128), F32),
        vm((16, PAD, 128), BF16),
        vm((16, PAD, 128), BF16),
        vm((16, PAD, 128), BF16),
        vm((16, PAD, 128), BF16),
        vm((2, TAB, TAB), BF16),
        vm((2, TAB, TAB), BF16),
        vm((TAB, TAB), BF16),
        vm((2, OWN, WAVES), F32),
        vm((2, 128, TAB), F32),
        vm((2, TAB, 128), F32),
        vm((CH, 768), BF16),
        vm((768, CH), BF16),
        vm((FIELDS, CH), BF16),
        vm((ROWS, LOCAL, HO), BF16),
        vm((ROWS + 2 * RIM, PAD, HP), F32),
        vm((ROWS, PAD, HP), BF16),
        vm((2, RIM, PAD, HP), BF16),
        vm((2, ROWS, 8, HP), F32),
        vm((2, ROWS, 8, HP), F32),
        vm((2, LATS, 8, CH), F32),
        vm((2, LATS, 8, CH), F32),
        vm((8, 8, 128), F32),
        vm((6, 3, 8, 128), F32),
        vm((8, 128), F32),
        vm((2, 8, 128), F32),
        vm((KS, KS, HO), F32),
        vm((KS, 8, HP), F32),
        vm((FIELDS, HO), BF16),
        vm((128, HP), BF16),
        vm((HO, 800), BF16),
        vm((HO, 800), BF16),
        vm((FIELDS, HO), BF16),
        vm((ROWS, LOCAL), jnp.int32),
        vm((8, 128), F32),
        vm((ROWS, PAD, HP), F32),
        vm((384, 768), BF16),
        vm((256, 128), BF16),
        vm((KS * 128, HP), BF16),
        vm((ROWS * PAD, KS * 128), BF16),
        vm((512, CH), BF16),
        vm((768, HO), BF16),
        vm((LATS * PAD, CH), F32),
        vm((LATS * PAD, CH), BF16),
        vm((PAD, 128), BF16),
        vm((6, PAD, 128), BF16),
        vm((SPAN, 64, PAD), BF16),
        vm((SPAN, 64, PAD), BF16),
        vm((LOCAL, LATS, CH), BF16),
        vm((ROWS, LOCAL, HO), BF16),
        vm((LATS, FIELDS, LOCAL), BF16),
        dma((15,)),
        dma((3,)),
        dma((16,)),
        dma((16,)),
        dma((16,)),
        dma((16,)),
        dma((6,)),
        dma((6,)),
        dma((2,)),
        dma((2,)),
        dma((2,)),
        dma((2,)),
        dma((2,)),
        dma((2,)),
        dma((2,)),
        dma((2,)),
        dma((6,)),
        dma((6,)),
        dma((4,)),
        dma((4,)),
    ]
    out = pl.pallas_call(
        functools.partial(body, bands, cols),
        out_shape=(
            jax.ShapeDtypeStruct((LOCAL, LATS, CH), BF16),
            jax.ShapeDtypeStruct((ROWS, LOCAL, HO), BF16),
            jax.ShapeDtypeStruct((LATS, FIELDS, LOCAL), BF16),
        ),
        in_specs=[any_spec] * 5 + [smem] * 3 + [any_spec] * 10,
        out_specs=(any_spec,) * 3,
        scratch_shapes=scratch,
        compiler_params=pltpu.CompilerParams(
            collective_id=0, has_side_effects=True, vmem_limit_bytes=56 * 1024 * 1024
        ),
    )(
        jnp.transpose(atm_state, (1, 0, 2)),
        jnp.transpose(spec_gain, (0, 2, 1)),
        mlp_in,
        mlp_out,
        jnp.transpose(flux_proj),
        jnp.transpose(pair_rows, (1, 2, 0)),
        jnp.transpose(pair_count),
        jnp.transpose(pair_weight, (0, 2, 1)),
        ocean_state,
        force_proj,
        depth_kernel,
        ocean_in,
        jnp.transpose(ocean_out),
        jnp.transpose(surf_proj),
        land_mask,
        *consts,
    )
    return (
        jnp.transpose(out[0], (1, 0, 2)),
        out[1],
        jnp.transpose(out[2], (0, 2, 1)),
    )


def solution(mesh):
    placed = (
        P("band", "col", None),
        P(None, None, "col"),
        P(),
        P(),
        P(),
        P(None, "band", None),
        P(None, "band"),
        P("band", None, None),
        P("band", "col", None),
        P(),
        P(),
        P(),
        P(),
        P(),
        P("band", "col"),
    )
    consts = tables()
    step = functools.partial(
        per_device, mesh.shape["band"], mesh.shape["col"], [jnp.asarray(t) for t in consts]
    )
    return jax.shard_map(
        step,
        mesh=mesh,
        in_specs=placed,
        out_specs=(P("band", "col", None), P("band", "col", None), P("band", "col", None)),
        check_vma=False,
    )
```

time: 119 us -> 51.1 us (0.43)
  starting transfers between devices: 46.3 us -> 0 us
  Pallas kernels: 0 us -> 45.4 us
  other arithmetic: 25.4 us -> 0 us
  matrix products: 16.1 us -> 0 us
  waiting for transfers between devices: 14.9 us -> 0 us
  local copies, waits for them, and re-layouts: 14.5 us -> 4.77 us
    pallas_call x0 -> x1, Pallas kernels: none -> 45.4 us  [per_device(): pl.pallas_call(functools.partial(body, bands, cols), out_shape=(jax.Shape...]
    ppermute x10 -> x0, starting transfers between devices: 32.1 us -> none  [the longest x6 20.9 us: passed_along(): return lax.ppermute(value, axis, pairs)]
    sin x1 -> x0, other arithmetic: 19.6 us -> none  [wave_table(): return jnp.concatenate([jnp.cos(angle), jnp.sin(angle)], axis=0)]
    all_to_all x2 -> x0, starting transfers between devices: 14.3 us -> none  [the longest x1 7.58 us: per_device(): lax.all_to_all(atm_state, 'col', split_axis=2, concat_axis=1, tiled=True)]
    dot_general x19 -> x0, matrix products: 9.44 us -> none  [the longest x1 2.95 us: per_device(): jnp.einsum('kl,akc->alc', table, filtered, precision=FAIR) * (2.0 / length)]
    ppermute x10 -> x0, waiting for transfers between devices: 7.93 us -> none  [the longest x6 3.35 us: passed_along(): return lax.ppermute(value, axis, pairs)]
    all_to_all x2 -> x0, waiting for transfers between devices: 6.92 us -> none  [the longest x1 6.92 us: per_device(): lax.all_to_all(zonal.astype(jnp.bfloat16), 'col', split_axis=1, concat_ax...]
    unnamed x2 -> x0, matrix products: 6.69 us -> none
  transfers between devices with their start and end apart: 12 -> 0, of which waited for: 5 -> 0; matrix products, arithmetic and copies ran while one was open for 19% -> 0% of each run, Pallas kernels for 0% -> 0%
where the time goes in v1:
time: 51.1 us; the launch traced here: 50.8 us
  Pallas kernels  45.4 us (89%)
  local copies, waits for them, and re-layouts  4.77 us (9%)
  between operations  0.65 us (1%)
    pallas_call x1, Pallas kernels, per_device(): pl.pallas_call(functools.partial(body, bands, cols), out_shape=(jax.Shape...  45.4 us
    unnamed x3, local copies, waits for them, and re-layouts  4.77 us

profile of v1, /device:TPU:1, one launch (start us, length us, event | category | flops | bytes accessed | tf_op | source)
XLA Modules:
  0.0 50.8 jit_solution(16107148857961478789)
XLA Ops:
  0.6 45.4 %shard_map.193 = (bf16[90,4,384]{2,1,0:T(4,128)(2,1)}, bf16[6,90,200]{2,1,0:T(8,128)(2,1)}, bf16[4,16,90]{2,1,0:T(8,128)(2,1)}) custom-call(bf16[90,4,384]{2,1,0:T(4,128)(2,1)} %bitcast.11, f32[2,24,720]{2,1,0:T(8,128)} %bitcast.13, bf16[384,768]{1,0:T(8,128)(2,1)} %w_in.1, bf16[768,384]{1,0:T(8,128)(2,1)} %w_out.1, bf16[16,384]{1,0:T(8,128)(2,1)} %bitcast.15, ...), custom_call_target="tpu_custom_call" | custom-call | tf_op jit(solution)/shard_map/pallas_call | solution.py:686
  46.0 1.8 %copy.24 = bf16[4,90,384]{2,0,1:T(4,128)(2,1)} copy(bf16[4,90,384]{2,0,1:T(4,128)(2,1)} %bitcast.12) | data formatting | bytes 552960
  47.8 1.7 %copy.25 = bf16[6,90,200]{2,1,0:T(8,128)(2,1)} copy(bf16[6,90,200]{2,1,0:T(8,128)(2,1)} %get-tuple-element.13) | data formatting | bytes 432000
  49.5 1.3 %copy.26 = bf16[4,90,16]{1,2,0:T(8,128)(2,1)} copy(bf16[4,90,16]{1,2,0:T(8,128)(2,1)} %bitcast.14) | data formatting | bytes 23040

commit v2 on v1

v2 whole, which is shorter than its diff:
```python
import functools

import jax
import jax.numpy as jnp
import numpy as np
from jax import lax
from jax.experimental import pallas as pl
from jax.experimental.pallas import tpu as pltpu
from jax.sharding import PartitionSpec as P

F32 = jnp.float32
BF16 = jnp.bfloat16
MESH = pl.DeviceIdType.MESH
ANY = pl.ANY

SPAN = 4
LATS = 4
SLOTS = 4
LON = 1440
WAVES = 720
LOCAL = 90
PAD = 96
RIM = 3
KS = 7
CH = 384
OWN = 24
HALF = LON // 2
BLOCKS = 8
TAB = BLOCKS * PAD
WPAD = TAB // 2
ROWS = 6
HO = 200
HP = 256
FIELDS = 16
NT = (((1,), (1,)), ((), ()))


def tables():
    place = np.arange(PAD)
    block = np.arange(BLOCKS)
    inside = np.broadcast_to(place < LOCAL, (BLOCKS, PAD)).reshape(-1)
    lon_in = (LOCAL * block[:, None] + place[None]).reshape(-1)
    rim = np.where(place < LOCAL + RIM, place, place - PAD)
    lon_out = (LOCAL * block[:, None] + rim[None]).reshape(-1)
    forward = np.zeros((2, TAB, TAB), np.float64)
    inverse = np.zeros((2, TAB, TAB), np.float64)
    deal = np.zeros((2 * WPAD, TAB), np.float64)
    count = WAVES // 2
    for parity in range(2):
        wave = 2 * np.arange(count) + parity
        angle = 2 * np.pi * (wave[:, None] * lon_in[None] % LON) / LON
        forward[parity, :count] = np.cos(angle) * inside
        forward[parity, WPAD : WPAD + count] = np.sin(angle) * inside
        angle = 2 * np.pi * (lon_out[:, None] * wave[None] % LON) / LON
        inverse[parity, :, :count] = np.cos(angle)
        inverse[parity, :, WPAD : WPAD + count] = np.sin(angle)
        deal[parity * WPAD + np.arange(count), wave] = 1.0
    return [t.astype(np.float32).astype(jnp.bfloat16) for t in (forward, inverse, deal)]


def iota(shape, axis):
    return lax.broadcasted_iota(jnp.int32, shape, axis)


def one_hot(condition):
    return jnp.where(condition, 1.0, 0.0).astype(BF16)


def dot(a, b):
    return jnp.dot(a, b, preferred_element_type=F32)


def dot_nt(a, b):
    return lax.dot_general(a, b, NT, preferred_element_type=F32)


def windows(tile):
    out = []
    for d in range(16):
        lo, hi = max(OWN * d, 128 * tile), min(OWN * d + OWN, 128 * tile + 128)
        if lo < hi:
            out.append((d, lo, hi - lo))
    return out


def body(
    bands,
    cols,
    atm,
    gain,
    w_in,
    w_out,
    flux_t,
    p_rows,
    p_count,
    p_weight,
    ocean,
    force,
    kernel_w,
    o_in,
    o_out_t,
    surf_t,
    land,
    tab_f,
    tab_i,
    deal,
    ao,
    oo,
    so,
    xv,
    st,
    x32,
    rolled,
    send1,
    recv1,
    send2,
    recv2,
    tf,
    ti,
    dl,
    gv,
    gx,
    gt,
    w1,
    w2,
    fpt,
    ocv,
    oc,
    obs,
    obr,
    ohs,
    ohr,
    ahs,
    ahr,
    sel,
    selr,
    wown,
    wr,
    kv,
    kp,
    fp,
    fpc,
    oin,
    oot,
    spt,
    lm,
    lmp,
    s0,
    biga,
    bigb,
    wst,
    xs,
    fxt,
    sxt,
    mx,
    nx,
    flx,
    flr,
    bks,
    bkr,
    waves,
    ld,
    a1s,
    a1r,
    a2s,
    a2r,
    sls,
    slr,
    ws,
    wrs,
    ohss,
    ohrs,
    obss,
    obrs,
    ahss,
    ahrs,
    fls,
    flrs,
    bss,
    brs,
):
    me = lax.axis_index("col")
    band = lax.axis_index("band")
    up_ok = jnp.where(band > 0, 1.0, 0.0).astype(F32)
    down_ok = jnp.where(band < bands - 1, 1.0, 0.0).astype(F32)

    def col_at(k):
        return lax.rem(me + k + cols, cols)

    def exists(k):
        return band >= -k if k < 0 else band < bands - k

    def load(src, dst, k):
        c = pltpu.make_async_copy(src, dst, ld.at[k])
        c.start()
        return c

    l_atm = load(atm, xv, 0)
    l_ocean = load(ocean, ocv, 1)
    l_force = load(force, fp, 2)
    l_kernel = load(kernel_w, kv, 3)
    l_gain = load(gain, gv, 4)
    l_deal = load(deal, dl, 5)
    l_tf = load(tab_f, tf, 6)
    l_flux = load(flux_t, fpt, 7)
    l_surf = load(surf_t, spt, 8)
    l_land = load(land, lm, 9)
    l_ti = load(tab_i, ti, 10)
    l_w1 = load(w_in, w1, 11)
    l_w2 = load(w_out, w2, 12)
    l_oin = load(o_in, oin, 13)
    l_oot = load(o_out_t, oot, 14)

    barrier = pltpu.get_barrier_semaphore()
    for k in range(1, cols):
        pl.semaphore_signal(barrier, inc=1, device_id={"col": col_at(k)}, device_id_type=MESH)
    for k in range(1, SPAN + 1):

        @pl.when(exists(k))
        def _():
            pl.semaphore_signal(barrier, inc=1, device_id={"band": band + k}, device_id_type=MESH)

    def remote(src, dst, send_sem, recv_sem, device):
        return pltpu.make_async_remote_copy(
            src_ref=src,
            dst_ref=dst,
            send_sem=send_sem,
            recv_sem=recv_sem,
            device_id=device,
            device_id_type=MESH,
        )

    def to_band(k, src, dst, send_sem, recv_sem):
        def make():
            return remote(src, dst, send_sem, recv_sem, {"band": band + k})

        def start():
            pl.when(exists(k))(lambda: make().start())

        def wait_send():
            pl.when(exists(k))(lambda: make().wait_send())

        def wait_recv():
            pl.when(exists(-k))(lambda: make().wait_recv())

        return start, wait_send, wait_recv

    def slots_to(o):
        return to_band(1 - o, sel.at[pl.ds(5 - o, 3)], selr.at[o], sls.at[o], slr.at[o])

    def weights_to(side):
        return to_band(1 - 2 * side, wown, wr.at[side], ws.at[side], wrs.at[side])

    def rim_to(side):
        src = obs.at[pl.ds(RIM * (1 - side), RIM)]
        return to_band(1 - 2 * side, src, obr.at[side], obss.at[side], obrs.at[side])

    def flux_to(o):
        return to_band(1 - o, flx, flr.at[o], fls.at[o], flrs.at[o])

    def back_to(o):
        return to_band(o, bks.at[o], bkr.at[o], bss.at[o], brs.at[o])

    lane = iota((PAD, 128), 1)

    def phase_pack():
        st[:, LATS * LOCAL :, :] = jnp.zeros((3, LATS * (PAD - LOCAL), 128), F32)
        for l in range(LOCAL):
            for t in range(3):
                cut = slice(128 * t, 128 * t + 128)
                st[t, LATS * l : LATS * l + LATS, :] = xv[l, :, cut].astype(F32)
        for a in range(LATS):
            for t in range(3):
                part = st.at[t][pl.ds(a, PAD, stride=LATS), :]
                x32[a, :, 128 * t : 128 * t + 128] = part
                rolled[a, t] = pltpu.roll(part, OWN * a, 1) if a else part
        for d in range(cols):
            out = jnp.zeros((PAD, 128), F32)
            for t in range(3):
                for e, lo, n in windows(t):
                    if e == d:
                        for a in range(LATS):
                            mask = ((lane - (lo + OWN * a)) & 127) < n
                            out = jnp.where(mask, rolled[a, t], out)
            send1[d] = out.astype(BF16)
        recv1[me] = send1[me]

    def phase_slots():
        row8 = iota((8, 128), 0)
        lane8 = iota((8, 128), 1)
        zero8 = jnp.zeros((8, 128), F32)
        for q in (0, 1, 6, 7):
            sel[q] = zero8
        for k in range(SPAN):
            other = band - k
            at = jnp.maximum(other, 0)
            used = jnp.where(other >= 0, p_count[0, at], 0)
            vec = zero8
            for p in range(SLOTS):
                target = jnp.where(p < used, SLOTS * p_rows[0, p, at] + p, -1)
                vec = jnp.where(lane8 == target, 1.0, vec)
            sel[5 - k] = vec
        vec = zero8
        for o in range(SPAN):
            at = jnp.minimum(band + o, bands - 1)
            for p in range(SLOTS):
                here = (lane8 // 16 == o) & (lane8 % SLOTS == p)
                for i in range(ROWS):
                    vec = jnp.where(here & (row8 == i), p_weight[i, p, at], vec)
        wown[...] = vec
        selr[1] = sel[4:7]
        for o in range(2, 6):

            @pl.when(jnp.logical_not(exists(o - 1)))
            def _():
                selr[o] = jnp.zeros((3, 8, 128), F32)
                flr[o] = jnp.zeros((PAD, 128), BF16)

        @pl.when(jnp.logical_not(exists(-1)))
        def _():
            selr[0] = jnp.zeros((3, 8, 128), F32)
            flr[0] = jnp.zeros((PAD, 128), BF16)
            wr[0] = zero8
            obr[0] = jnp.zeros((RIM, PAD, HP), BF16)

        @pl.when(jnp.logical_not(exists(1)))
        def _():
            wr[1] = zero8
            obr[1] = jnp.zeros((RIM, PAD, HP), BF16)

        for o in range(1, SPAN):

            @pl.when(jnp.logical_not(exists(-o)))
            def _():
                bkr[o] = jnp.zeros((64, PAD), BF16)

    def phase_rims():
        oc[RIM : RIM + ROWS] = jnp.zeros((ROWS, PAD, HP), F32)
        oc[RIM : RIM + ROWS, 0:LOCAL, 0:HO] = ocv[...].astype(F32)
        for i in range(ROWS):
            ohs[0, i] = pltpu.roll(oc[RIM + i, 0:8, :], 2, 0)
            ohs[1, i] = pltpu.roll(oc[RIM + i, 80:96, :], 6, 0)[8:16]
        for a in range(LATS):
            ahs[0, a] = pltpu.roll(x32[a, 0:8, :], 2, 0)
            ahs[1, a] = pltpu.roll(x32[a, 80:96, :], 6, 0)[8:16]

    def phase_gains():
        gx[...] = jnp.zeros(gx.shape, F32)
        for a in range(LATS):
            for q in range(OWN // 8):
                row = pl.multiple_of(lax.rem(OWN * (me + a) + 8 * q, 128), 8)
                gx[:, pl.ds(row, 8), 0:WAVES] = gv[:, 8 * q : 8 * q + 8, :] * (2.0 / LON)
        for part in range(2):
            g = gx[part]
            high = g.astype(BF16)
            low = (g - high.astype(F32)).astype(BF16)
            both = dot_nt(dl[...], jnp.concatenate([high, low], axis=0))
            gt[part] = both[:, :128] + both[:, 128:]

    def phase_weights():
        kp[...] = jnp.zeros(kp.shape, F32)
        kp[:, 0:KS, 0:HO] = kv[...]
        f32_force = fp[...].astype(F32)
        wst[...] = jnp.zeros(wst.shape, BF16)
        fpc[...] = jnp.zeros(fpc.shape, BF16)
        for dj in range(KS):
            for di in range(KS):
                at = 128 * dj + FIELDS * di
                wst[at : at + FIELDS, 0:HO] = (f32_force * kp[di, dj : dj + 1, 0:HO]).astype(BF16)
        fpc[FIELDS * RIM : FIELDS * RIM + FIELDS, 0:HO] = fp[...]

        r, f = iota((512, FIELDS), 0), iota((512, FIELDS), 1)
        spread = one_hot((r % 64 // 16 == r // 128) & (r % 16 == f))
        fxt[...] = dot(spread, fpt[...]).astype(BF16)
        r, f = iota((768, FIELDS), 0), iota((768, FIELDS), 1)
        spread = one_hot((r % 128 // 16 == r // 128) & (r % 16 == f))
        sxt[...] = dot(spread, spt[...]).astype(BF16)
        lmp[...] = jnp.zeros(lmp.shape, F32)
        lmp[0:ROWS, 0:LOCAL] = lm[...].astype(F32)

    def phase_ocean_rim():
        sub = iota((8, HP), 0)
        for i in range(ROWS):
            tile = oc[RIM + i, 88:96, :]
            oc[RIM + i, 88:96, :] = jnp.where(
                sub < 2, tile, jnp.where(sub < 5, ohr[0, i], ohr[1, i])
            )
        obs[...] = oc[RIM : RIM + ROWS].astype(BF16)

    def phase_matrices():
        blocks = []
        for b in range(3):
            chosen = selr[0, b]
            for o in range(1, 6):
                chosen = chosen + pltpu.roll(selr[o, b], 16 * o, 1)
            if b == 0:
                blocks.append(wr[0] * chosen * up_ok)
            elif b == 1:
                blocks.append(pltpu.roll(wown[...], 16, 1) * chosen)
            else:
                blocks.append(pltpu.roll(wr[1], 32, 1) * chosen * down_ok)
        slots = jnp.concatenate(blocks, axis=0).astype(BF16)
        r, c_ = iota((384, 128), 0), iota((384, 128), 1)
        by_row = dot_nt(one_hot(r // 16 == c_ // 4), slots).astype(BF16)
        r, c_ = iota((24, 768), 0), iota((24, 768), 1)
        tap = c_ % 128 // 16
        need = c_ // 128 + tap
        has = r % 8 + jnp.where(r < 8, -RIM, jnp.where(r < 16, RIM, RIM + ROWS))
        legal = (
            (tap < KS)
            & ((r >= 8) | (r % 8 >= ROWS - RIM))
            & (r % 8 < ROWS)
            & ((r < 16) | (r % 8 < RIM))
        )
        spread = one_hot(legal & (need == has))
        r, c_ = iota((384, 768), 0), iota((384, 768), 1)
        biga[...] = jnp.where(r % 16 == c_ % 16, dot(by_row, spread), 0.0).astype(BF16)
        r, c_ = iota((128, 24), 0), iota((128, 24), 1)
        by_own = dot(one_hot((c_ - 8 == r // 16) & (r // 16 < ROWS)), slots).astype(BF16)
        r, c_ = iota((256, 128), 0), iota((256, 128), 1)
        full = dot_nt(one_hot(c_ // 4 == 4 * (r // 64 + 1) + r % 64 // 16), by_own)
        bigb[...] = jnp.where(r % 16 == c_ % 16, full, 0.0).astype(BF16)

    def phase_spectra():
        first = recv1[0:BLOCKS].reshape(TAB, 128).astype(F32)
        second = recv1[BLOCKS : 2 * BLOCKS].reshape(TAB, 128).astype(F32)
        for parity in range(2):
            mix = first - second if parity else first + second
            spec = dot(tf[parity], mix.astype(BF16))
            real, imag = spec[:WPAD], spec[WPAD:]
            rows = slice(parity * WPAD, parity * WPAD + WPAD)
            g_real, g_imag = gt[0, rows], gt[1, rows]
            waves[parity, :WPAD] = (g_real * real + g_imag * imag).astype(BF16)
            waves[parity, WPAD:] = (g_real * imag - g_imag * real).astype(BF16)

    chunk = 2

    def phase_inverse(k):
        parts = BLOCKS // chunk
        q = lax.rem(me // chunk + k, parts)
        rows = pl.ds(pl.multiple_of(q * (chunk * PAD), chunk * PAD), chunk * PAD)
        even = dot(ti[0, rows, :], waves[0])
        odd = dot(ti[1, rows, :], waves[1])
        send2[pl.ds(q * chunk, chunk)] = (even + odd).astype(BF16).reshape(chunk, PAD, 128)
        send2[pl.ds(q * chunk + BLOCKS, chunk)] = (
            (even - odd).astype(BF16).reshape(chunk, PAD, 128)
        )
        return q

    def phase_stencil():
        oc[0:RIM] = obr[0].astype(F32) * up_ok
        oc[RIM + ROWS :] = obr[1].astype(F32) * down_ok

        def stencil_row(i, carry):
            for t in range(HP // 128):
                cut = slice(128 * t, 128 * t + 128)
                total = None
                for dj in range(KS):
                    line = None
                    for di in range(KS):
                        term = kp[di, dj : dj + 1, cut] * oc[i + di, :, cut]
                        line = term if line is None else line + term
                    shift = (RIM - dj) % PAD
                    line = pltpu.roll(line, shift, 0) if shift else line
                    total = line if total is None else total + line
                s0[i, :, cut] = total
            return carry

        lax.fori_loop(0, ROWS, stencil_row, 0)

    def phase_atm_rim():
        sub = iota((8, CH), 0)
        for a in range(LATS):
            tile = x32[a, 88:96, :]
            x32[a, 88:96, :] = jnp.where(sub < 2, tile, jnp.where(sub < 5, ahr[0, a], ahr[1, a]))

    def phase_unpack():
        for a in range(LATS):
            for t in range(3):
                cut = slice(128 * t, 128 * t + 128)
                zonal = jnp.zeros((PAD, 128), F32)
                for d, lo, n in windows(t):
                    mask = ((lane - (lo + OWN * a)) & 127) < n
                    zonal = jnp.where(mask, recv2[d].astype(F32), zonal)
                if a:
                    zonal = pltpu.roll(zonal, 128 - OWN * a, 1)
                mx[a * PAD : a * PAD + PAD, cut] = x32[a, :, cut] + zonal

    def phase_atm():
        mixed = mx[...]
        centred = mixed - jnp.mean(mixed, axis=-1, keepdims=True)
        spread = jnp.mean(centred * centred, axis=-1, keepdims=True)
        normed = (centred * lax.rsqrt(spread + 1e-05)).astype(BF16)
        inner = jax.nn.gelu(dot(normed, w1[...])).astype(BF16)
        nx[...] = (mx[...] + dot(inner, w2[...])).astype(BF16)
        flux = None
        for a in range(LATS):
            term = dot_nt(nx[a * PAD : a * PAD + PAD, :], fxt[128 * a : 128 * a + 128, :])
            flux = term if flux is None else flux + term
        flx[...] = flux.astype(BF16)
        flr[1] = flx[...]

    def phase_atm_out():
        for t in range(3):
            cut = slice(128 * t, 128 * t + 128)
            for a in range(LATS):
                part = nx[a * PAD : a * PAD + PAD, cut].astype(F32)
                st.at[t][pl.ds(a, PAD, stride=LATS), :] = part
            for l in range(LOCAL):
                ao[l, :, cut] = st[t, LATS * l : LATS * l + LATS, :].astype(BF16)

    def phase_forcing():
        low = iota((PAD, 128), 1) < 64
        tiles = [
            jnp.where(low, flr[2 * q].astype(F32), flr[2 * q + 1].astype(F32)).astype(BF16)
            for q in range(3)
        ]
        forcing = dot(jnp.concatenate(tiles, axis=1), biga[...])
        for i in range(ROWS):
            part = forcing[:, 128 * i : 128 * i + 128]
            for dj in range(KS):
                shift = (RIM - dj) % PAD
                turned = pltpu.roll(part, shift, 0) if shift else part
                xs[PAD * i : PAD * i + PAD, 128 * dj : 128 * dj + 128] = turned.astype(BF16)

    def phase_ocean():
        r, c_ = iota((128, 128), 0), iota((128, 128), 1)
        sea = dot_nt(one_hot(r == c_), lmp[...].astype(BF16))
        rows = ROWS * PAD
        stencil = (dot(xs[...], wst[...]) + s0[...].reshape(rows, HP))[:, :HO]
        centred = stencil - jnp.mean(stencil, axis=-1, keepdims=True)
        spread = jnp.mean(centred * centred, axis=-1, keepdims=True)
        onorm = (centred * lax.rsqrt(spread + 1e-05)).astype(BF16)
        hidden = jax.nn.gelu(dot(onorm, oin[...])).astype(BF16)
        change = dot_nt(hidden, oot[...])
        pushed = dot(xs[:, 128 * RIM : 128 * RIM + 128], fpc[...])
        lifted = (oc[RIM : RIM + ROWS].reshape(rows, HP) + pushed)[:, :HO].astype(BF16).astype(F32)
        result = lifted + change
        surface = None
        for i in range(ROWS):
            part = (result[PAD * i : PAD * i + PAD] * sea[0:PAD, i : i + 1]).astype(BF16)
            oo[i] = part[:LOCAL]
            term = dot_nt(part, sxt[128 * i : 128 * i + 128, :])
            surface = term if surface is None else surface + term
        back = dot_nt(bigb[...], surface.astype(BF16)).astype(BF16)
        for o in range(SPAN):
            bks[o] = back[64 * o : 64 * o + 64]

    def phase_sum():
        total = bks[0].astype(F32)
        for o in range(1, SPAN):
            total = total + bkr[o].astype(F32)
        so[...] = total.reshape(LATS, FIELDS, PAD)[:, :, :LOCAL].astype(BF16)

    l_atm.wait()
    phase_pack()
    phase_slots()
    pl.semaphore_wait(barrier, cols - 1 + jnp.minimum(band, SPAN))

    a1 = []
    for k in range(1, cols):
        d = col_at(k)
        c = remote(send1.at[d], recv1.at[me], a1s.at[k], a1r.at[k], {"col": d})
        c.start()
        a1.append(c)
    for o in range(2, 6):
        slots_to(o)[0]()
    weights_to(1)[0]()
    l_ocean.wait()
    phase_rims()
    oh = []
    for side, k in ((0, -1), (1, 1)):
        c = remote(ohs.at[side], ohr.at[side], ohss.at[side], ohrs.at[side], {"col": col_at(k)})
        c.start()
        oh.append(c)

    l_gain.wait()
    l_deal.wait()
    phase_gains()
    l_force.wait()
    l_kernel.wait()
    l_flux.wait()
    l_surf.wait()
    l_land.wait()
    phase_weights()

    for o in range(2, 6):
        slots_to(o)[2]()
    weights_to(1)[2]()
    slots_to(0)[0]()
    weights_to(0)[0]()
    for c in oh:
        c.wait()
    phase_ocean_rim()
    rim_to(0)[0]()
    rim_to(1)[0]()

    l_tf.wait()
    for c in a1:
        c.wait_recv()
    phase_spectra()
    ah = []
    for side, k in ((0, -1), (1, 1)):
        c = remote(ahs.at[side], ahr.at[side], ahss.at[side], ahrs.at[side], {"col": col_at(k)})
        c.start()
        ah.append(c)
    l_ti.wait()
    for k in range(BLOCKS // chunk):
        q = phase_inverse(k)
        for n in range(2 * chunk):
            to = q * chunk + n % chunk + BLOCKS * (n // chunk)
            step = lax.rem(to - me + cols, cols)

            @pl.when(to != me)
            def _():
                remote(
                    send2.at[to], recv2.at[me], a2s.at[step], a2r.at[step], {"col": to}
                ).start()

    recv2[me] = send2[me]

    slots_to(0)[2]()
    weights_to(0)[2]()
    phase_matrices()
    rim_to(0)[2]()
    rim_to(1)[2]()
    phase_stencil()

    for c in ah:
        c.wait()
    phase_atm_rim()
    for k in range(1, cols):
        remote(send2.at[0], recv2.at[0], a2s.at[k], a2r.at[k], {"col": col_at(k)}).wait_recv()
    phase_unpack()
    l_w1.wait()
    l_w2.wait()
    phase_atm()
    for o in (5, 4, 3, 2, 0):
        flux_to(o)[0]()
    phase_atm_out()

    l_oin.wait()
    l_oot.wait()
    for o in (0, 2, 3, 4, 5):
        flux_to(o)[2]()
    phase_forcing()
    phase_ocean()
    for o in range(1, SPAN):
        back_to(o)[0]()
    for o in range(1, SPAN):
        back_to(o)[2]()
    phase_sum()

    for c in a1:
        c.wait_send()
    for k in range(1, cols):
        remote(send2.at[0], recv2.at[0], a2s.at[k], a2r.at[k], {"col": col_at(k)}).wait_send()
    for o in (0, 2, 3, 4, 5):
        slots_to(o)[1]()
        flux_to(o)[1]()
    for side in range(2):
        weights_to(side)[1]()
        rim_to(side)[1]()
    for o in range(1, SPAN):
        back_to(o)[1]()


def store(a, b, c, a_out, b_out, c_out, sems):
    copies = [
        pltpu.make_async_copy(x, y, sems.at[k])
        for k, (x, y) in enumerate(((a, a_out), (b, b_out), (c, c_out)))
    ]
    for x in copies:
        x.start()
    for x in copies:
        x.wait()


def per_device(
    bands,
    cols,
    consts,
    atm_state,
    spec_gain,
    mlp_in,
    mlp_out,
    flux_proj,
    pair_rows,
    pair_count,
    pair_weight,
    ocean_state,
    force_proj,
    depth_kernel,
    ocean_in,
    ocean_out,
    surf_proj,
    land_mask,
):
    any_spec = pl.BlockSpec(memory_space=ANY)
    smem = pl.BlockSpec(memory_space=pltpu.SMEM)
    vm = pltpu.VMEM
    dma = pltpu.SemaphoreType.DMA
    scratch = [
        vm((LOCAL, LATS, CH), BF16),
        vm((3, LATS * PAD, 128), F32),
        vm((LATS, PAD, CH), F32),
        vm((LATS, 3, PAD, 128), F32),
        vm((16, PAD, 128), BF16),
        vm((16, PAD, 128), BF16),
        vm((16, PAD, 128), BF16),
        vm((16, PAD, 128), BF16),
        vm((2, TAB, TAB), BF16),
        vm((2, TAB, TAB), BF16),
        vm((TAB, TAB), BF16),
        vm((2, OWN, WAVES), F32),
        vm((2, 128, TAB), F32),
        vm((2, TAB, 128), F32),
        vm((CH, 768), BF16),
        vm((768, CH), BF16),
        vm((FIELDS, CH), BF16),
        vm((ROWS, LOCAL, HO), BF16),
        vm((ROWS + 2 * RIM, PAD, HP), F32),
        vm((ROWS, PAD, HP), BF16),
        vm((2, RIM, PAD, HP), BF16),
        vm((2, ROWS, 8, HP), F32),
        vm((2, ROWS, 8, HP), F32),
        vm((2, LATS, 8, CH), F32),
        vm((2, LATS, 8, CH), F32),
        vm((8, 8, 128), F32),
        vm((6, 3, 8, 128), F32),
        vm((8, 128), F32),
        vm((2, 8, 128), F32),
        vm((KS, KS, HO), F32),
        vm((KS, 8, HP), F32),
        vm((FIELDS, HO), BF16),
        vm((128, HP), BF16),
        vm((HO, 800), BF16),
        vm((HO, 800), BF16),
        vm((FIELDS, HO), BF16),
        vm((ROWS, LOCAL), jnp.int32),
        vm((8, 128), F32),
        vm((ROWS, PAD, HP), F32),
        vm((384, 768), BF16),
        vm((256, 128), BF16),
        vm((KS * 128, HP), BF16),
        vm((ROWS * PAD, KS * 128), BF16),
        vm((512, CH), BF16),
        vm((768, HO), BF16),
        vm((LATS * PAD, CH), F32),
        vm((LATS * PAD, CH), BF16),
        vm((PAD, 128), BF16),
        vm((6, PAD, 128), BF16),
        vm((SPAN, 64, PAD), BF16),
        vm((SPAN, 64, PAD), BF16),
        vm((2, TAB, 128), BF16),
        dma((15,)),
        dma((16,)),
        dma((16,)),
        dma((16,)),
        dma((16,)),
        dma((6,)),
        dma((6,)),
        dma((2,)),
        dma((2,)),
        dma((2,)),
        dma((2,)),
        dma((2,)),
        dma((2,)),
        dma((2,)),
        dma((2,)),
        dma((6,)),
        dma((6,)),
        dma((4,)),
        dma((4,)),
    ]
    shapes = (
        jax.ShapeDtypeStruct((LOCAL, LATS, CH), BF16),
        jax.ShapeDtypeStruct((ROWS, LOCAL, HO), BF16),
        jax.ShapeDtypeStruct((LATS, FIELDS, LOCAL), BF16),
    )
    out = pl.pallas_call(
        functools.partial(body, bands, cols),
        out_shape=tuple(vm(x.shape, x.dtype) for x in shapes),
        in_specs=[any_spec] * 5 + [smem] * 3 + [any_spec] * 10,
        out_specs=(pl.BlockSpec(memory_space=vm),) * 3,
        scratch_shapes=scratch,
        compiler_params=pltpu.CompilerParams(
            collective_id=0, has_side_effects=True, vmem_limit_bytes=56 * 1024 * 1024
        ),
    )(
        jnp.transpose(atm_state, (1, 0, 2)),
        jnp.transpose(spec_gain, (0, 2, 1)),
        mlp_in,
        mlp_out,
        jnp.transpose(flux_proj),
        jnp.transpose(pair_rows, (1, 2, 0)),
        jnp.transpose(pair_count),
        jnp.transpose(pair_weight, (0, 2, 1)),
        ocean_state,
        force_proj,
        depth_kernel,
        ocean_in,
        jnp.transpose(ocean_out),
        jnp.transpose(surf_proj),
        land_mask,
        *consts,
    )
    out = pl.pallas_call(
        store,
        out_shape=shapes,
        in_specs=[pl.BlockSpec(memory_space=vm)] * 3,
        out_specs=(any_spec,) * 3,
        scratch_shapes=[dma((3,))],
    )(*out)
    return (
        jnp.transpose(out[0], (1, 0, 2)),
        out[1],
        jnp.transpose(out[2], (0, 2, 1)),
    )


def solution(mesh):
    placed = (
        P("band", "col", None),
        P(None, None, "col"),
        P(),
        P(),
        P(),
        P(None, "band", None),
        P(None, "band"),
        P("band", None, None),
        P("band", "col", None),
        P(),
        P(),
        P(),
        P(),
        P(),
        P("band", "col"),
    )
    consts = tables()
    step = functools.partial(
        per_device, mesh.shape["band"], mesh.shape["col"], [jnp.asarray(t) for t in consts]
    )
    return jax.shard_map(
        step,
        mesh=mesh,
        in_specs=placed,
        out_specs=(P("band", "col", None), P("band", "col", None), P("band", "col", None)),
        check_vma=False,
    )
```

time: 51.1 us -> 42.1 us (0.82)
  the two profiles are of different devices: /device:TPU:1 before, /device:TPU:129 now
where the time goes in v2:
time: 42.1 us; the launch traced here: 41.9 us
  Pallas kernels  39.3 us (93%)
  local copies, waits for them, and re-layouts  2 us (5%)
  between operations  0.66 us (2%)
    pallas_call x1, Pallas kernels, per_device(): pl.pallas_call(functools.partial(body, bands, cols), out_shape=tuple((vm(...  37.4 us
    unnamed x6, local copies, waits for them, and re-layouts  2 us
    pallas_call x1, Pallas kernels, per_device(): pl.pallas_call(store, out_shape=shapes, in_specs=[pl.BlockSpec(memory_spa...  1.88 us

profile of v2, /device:TPU:129, one launch (start us, length us, event | category | flops | bytes accessed | tf_op | source)
XLA Modules:
  0.0 41.9 jit_solution(7953618754108339508)
XLA Ops:
  0.6 37.4 %shard_map.193 = (bf16[90,4,384]{2,1,0:T(4,128)(2,1)S(1)}, bf16[6,90,200]{2,1,0:T(8,128)(2,1)S(1)}, bf16[4,16,90]{2,1,0:T(8,128)(2,1)S(1)}) custom-call(bf16[90,4,384]{2,1,0:T(4,128)(2,1)} %bitcast.11, f32[2,24,720]{2,1,0:T(8,128)} %bitcast.12, bf16[384,768]{1,0:T(8,128)(2,1)} %w_in.1, bf16[768,384]{1,0:T(8,128)(2,1)} %w_out.1, bf16[16,384]{1,0:T(8,128)(2,1)} %bitcast.13, ...), custom_call_target="tpu_custom_call" | custom-call | tf_op jit(solution)/shard_map/pallas_call | solution.py:781
  38.0 0.0 copy-start
  38.1 0.7 %copy-done = bf16[6,90,200]{2,1,0:T(8,128)(2,1)} copy-done((bf16[6,90,200]{2,1,0:T(8,128)(2,1)}, bf16[6,90,200]{2,1,0:T(8,128)(2,1)S(1)}, u32[]{:S(2)}) %copy-start) | copy-done | bytes 216024
  38.8 0.0 copy-start.1
  38.8 0.7 %copy-done.1 = bf16[90,4,384]{2,1,0:T(4,128)(2,1)} copy-done((bf16[90,4,384]{2,1,0:T(4,128)(2,1)}, bf16[90,4,384]{2,1,0:T(4,128)(2,1)S(1)}, u32[]{:S(2)}) %copy-start.1) | copy-done | bytes 276504
  39.5 0.0 copy-start.2
  39.5 0.6 %copy-done.2 = bf16[4,16,90]{2,1,0:T(8,128)(2,1)} copy-done((bf16[4,16,90]{2,1,0:T(8,128)(2,1)}, bf16[4,16,90]{2,1,0:T(8,128)(2,1)S(1)}, u32[]{:S(2)}) %copy-start.2) | copy-done | bytes 11544
  40.1 1.9 %shard_map.194 = (bf16[90,4,384]{2,1,0:T(4,128)(2,1)}, bf16[6,90,200]{2,1,0:T(8,128)(2,1)}, bf16[4,16,90]{2,1,0:T(8,128)(2,1)}) custom-call(bf16[90,4,384]{2,1,0:T(4,128)(2,1)} %copy-done.1, bf16[6,90,200]{2,1,0:T(8,128)(2,1)} %copy-done, bf16[4,16,90]{2,1,0:T(8,128)(2,1)} %copy-done.2), custom_call_target="tpu_custom_call" | custom-call | tf_op jit(solution)/shard_map/pallas_call | solution.py:808
Async XLA Ops:
  38.0 0.7 %copy-start = (bf16[6,90,200]{2,1,0:T(8,128)(2,1)}, bf16[6,90,200]{2,1,0:T(8,128)(2,1)S(1)}, u32[]{:S(2)}) copy-start(bf16[6,90,200]{2,1,0:T(8,128)(2,1)S(1)} %get-tuple-element.10.b) | copy-start | bytes 648004
  38.8 0.7 %copy-start.1 = (bf16[90,4,384]{2,1,0:T(4,128)(2,1)}, bf16[90,4,384]{2,1,0:T(4,128)(2,1)S(1)}, u32[]{:S(2)}) copy-start(bf16[90,4,384]{2,1,0:T(4,128)(2,1)S(1)} %get-tuple-element.9.a) | copy-start | bytes 829444
  39.5 0.6 %copy-start.2 = (bf16[4,16,90]{2,1,0:T(8,128)(2,1)}, bf16[4,16,90]{2,1,0:T(8,128)(2,1)S(1)}, u32[]{:S(2)}) copy-start(bf16[4,16,90]{2,1,0:T(8,128)(2,1)S(1)} %get-tuple-element.11.c) | copy-start | bytes 34564

commit v3 on v2

--- a/solution.py
+++ b/solution.py
@@ -91,9 +91,9 @@
     w_in,
     w_out,
     flux_t,
-    p_rows,
-    p_count,
-    p_weight,
+    pair_rows,
+    pair_count,
+    pair_weight,
     ocean,
     force,
     kernel_w,
@@ -128,10 +128,8 @@
     oc,
     obs,
     obr,
-    ohs,
-    ohr,
-    ahs,
-    ahr,
+    side_s,
+    side_r,
     sel,
     selr,
     wown,
@@ -159,6 +157,9 @@
     bks,
     bkr,
     waves,
+    p_rows,
+    p_count,
+    p_weight,
     ld,
     a1s,
     a1r,
@@ -168,12 +169,10 @@
     slr,
     ws,
     wrs,
-    ohss,
-    ohrs,
+    sds,
+    sdr,
     obss,
     obrs,
-    ahss,
-    ahrs,
     fls,
     flrs,
     bss,
@@ -187,6 +186,14 @@
     def col_at(k):
         return lax.rem(me + k + cols, cols)
 
+    def away(k):
+        return min(k // 4, 4 - k // 4) + min(k % 4, 4 - k % 4)
+
+    partners = [
+        lax.rem(me // 4 + k // 4, 4) * 4 + lax.rem(me % 4 + k % 4, 4)
+        for k in sorted(range(1, cols), key=lambda k: -away(k))
+    ]
+
     def exists(k):
         return band >= -k if k < 0 else band < bands - k
 
@@ -196,6 +203,9 @@
         return c
 
     l_atm = load(atm, xv, 0)
+    l_rows = load(pair_rows, p_rows, 15)
+    l_count = load(pair_count, p_count, 16)
+    l_weight = load(pair_weight, p_weight, 17)
     l_ocean = load(ocean, ocv, 1)
     l_force = load(force, fp, 2)
     l_kernel = load(kernel_w, kv, 3)
@@ -212,8 +222,8 @@
     l_oot = load(o_out_t, oot, 14)
 
     barrier = pltpu.get_barrier_semaphore()
-    for k in range(1, cols):
-        pl.semaphore_signal(barrier, inc=1, device_id={"col": col_at(k)}, device_id_type=MESH)
+    for d in partners:
+        pl.semaphore_signal(barrier, inc=1, device_id={"col": d}, device_id_type=MESH)
     for k in range(1, SPAN + 1):
 
         @pl.when(exists(k))
@@ -337,12 +347,26 @@
     def phase_rims():
         oc[RIM : RIM + ROWS] = jnp.zeros((ROWS, PAD, HP), F32)
         oc[RIM : RIM + ROWS, 0:LOCAL, 0:HO] = ocv[...].astype(F32)
-        for i in range(ROWS):
-            ohs[0, i] = pltpu.roll(oc[RIM + i, 0:8, :], 2, 0)
-            ohs[1, i] = pltpu.roll(oc[RIM + i, 80:96, :], 6, 0)[8:16]
-        for a in range(LATS):
-            ahs[0, a] = pltpu.roll(x32[a, 0:8, :], 2, 0)
-            ahs[1, a] = pltpu.roll(x32[a, 80:96, :], 6, 0)[8:16]
+        row = iota((16, HP), 0)
+        for b in range(2):
+            for side in range(2):
+                out = jnp.zeros((16, HP), F32)
+                for q in range(3):
+                    i = RIM + 3 * b + q
+                    part = oc[i, 0:16, :] if side == 0 else oc[i, 80:96, :]
+                    shift = (RIM * q - (0 if side == 0 else 7)) % 16
+                    part = pltpu.roll(part, shift, 0) if shift else part
+                    out = jnp.where((row >= RIM * q) & (row < RIM * q + RIM), part, out)
+                side_s[side, :, HP * b : HP * b + HP] = out.astype(BF16)
+        row = iota((16, CH), 0)
+        for side in range(2):
+            out = jnp.zeros((16, CH), F32)
+            for a in range(LATS):
+                part = x32[a, 0:16, :] if side == 0 else x32[a, 80:96, :]
+                shift = (RIM * a - (0 if side == 0 else 7)) % 16
+                part = pltpu.roll(part, shift, 0) if shift else part
+                out = jnp.where((row >= RIM * a) & (row < RIM * a + RIM), part, out)
+            side_s[side, :, 2 * HP :] = out.astype(BF16)
 
     def phase_gains():
         gx[...] = jnp.zeros(gx.shape, F32)
@@ -378,13 +402,19 @@
         lmp[...] = jnp.zeros(lmp.shape, F32)
         lmp[0:ROWS, 0:LOCAL] = lm[...].astype(F32)
 
+    def with_rim(own, right, left, row, k):
+        right = pltpu.roll(right, (10 - RIM * k) % 16, 0)
+        left = pltpu.roll(left, (13 - RIM * k) % 16, 0)
+        return jnp.where(row < 10, own, jnp.where(row < 13, right, left))
+
     def phase_ocean_rim():
-        sub = iota((8, HP), 0)
-        for i in range(ROWS):
-            tile = oc[RIM + i, 88:96, :]
-            oc[RIM + i, 88:96, :] = jnp.where(
-                sub < 2, tile, jnp.where(sub < 5, ohr[0, i], ohr[1, i])
-            )
+        row = iota((16, HP), 0)
+        for b in range(2):
+            cut = slice(HP * b, HP * b + HP)
+            right, left = side_r[0, :, cut].astype(F32), side_r[1, :, cut].astype(F32)
+            for q in range(3):
+                i = RIM + 3 * b + q
+                oc[i, 80:96, :] = with_rim(oc[i, 80:96, :], right, left, row, q)
         obs[...] = oc[RIM : RIM + ROWS].astype(BF16)
 
     def phase_matrices():
@@ -437,7 +467,7 @@
 
     def phase_inverse(k):
         parts = BLOCKS // chunk
-        q = lax.rem(me // chunk + k, parts)
+        q = lax.rem(me // chunk + k + 1, parts)
         rows = pl.ds(pl.multiple_of(q * (chunk * PAD), chunk * PAD), chunk * PAD)
         even = dot(ti[0, rows, :], waves[0])
         odd = dot(ti[1, rows, :], waves[1])
@@ -447,9 +477,11 @@
         )
         return q
 
-    def phase_stencil():
-        oc[0:RIM] = obr[0].astype(F32) * up_ok
-        oc[RIM + ROWS :] = obr[1].astype(F32) * down_ok
+    def phase_stencil(half):
+        if half:
+            oc[RIM + ROWS :] = obr[1].astype(F32) * down_ok
+        else:
+            oc[0:RIM] = obr[0].astype(F32) * up_ok
 
         def stencil_row(i, carry):
             for t in range(HP // 128):
@@ -466,13 +498,13 @@
                 s0[i, :, cut] = total
             return carry
 
-        lax.fori_loop(0, ROWS, stencil_row, 0)
+        lax.fori_loop(RIM * half, RIM * half + RIM, stencil_row, 0)
 
     def phase_atm_rim():
-        sub = iota((8, CH), 0)
+        row = iota((16, CH), 0)
+        right, left = side_r[0, :, 2 * HP :].astype(F32), side_r[1, :, 2 * HP :].astype(F32)
         for a in range(LATS):
-            tile = x32[a, 88:96, :]
-            x32[a, 88:96, :] = jnp.where(sub < 2, tile, jnp.where(sub < 5, ahr[0, a], ahr[1, a]))
+            x32[a, 80:96, :] = with_rim(x32[a, 80:96, :], right, left, row, a)
 
     def phase_unpack():
         for a in range(LATS):
@@ -554,25 +586,28 @@
 
     l_atm.wait()
     phase_pack()
+    l_rows.wait()
+    l_count.wait()
+    l_weight.wait()
     phase_slots()
+    l_ocean.wait()
+    phase_rims()
     pl.semaphore_wait(barrier, cols - 1 + jnp.minimum(band, SPAN))
 
     a1 = []
-    for k in range(1, cols):
-        d = col_at(k)
-        c = remote(send1.at[d], recv1.at[me], a1s.at[k], a1r.at[k], {"col": d})
+    for d in partners:
+        step = lax.rem(d - me + cols, cols)
+        c = remote(send1.at[d], recv1.at[me], a1s.at[step], a1r.at[step], {"col": d})
         c.start()
         a1.append(c)
+    sides = []
+    for side, k in ((0, -1), (1, 1)):
+        c = remote(side_s.at[side], side_r.at[side], sds.at[side], sdr.at[side], {"col": col_at(k)})
+        c.start()
+        sides.append(c)
+    weights_to(1)[0]()
     for o in range(2, 6):
         slots_to(o)[0]()
-    weights_to(1)[0]()
-    l_ocean.wait()
-    phase_rims()
-    oh = []
-    for side, k in ((0, -1), (1, 1)):
-        c = remote(ohs.at[side], ohr.at[side], ohss.at[side], ohrs.at[side], {"col": col_at(k)})
-        c.start()
-        oh.append(c)
 
     l_gain.wait()
     l_deal.wait()
@@ -583,27 +618,16 @@
     l_surf.wait()
     l_land.wait()
     phase_weights()
-
-    for o in range(2, 6):
-        slots_to(o)[2]()
-    weights_to(1)[2]()
-    slots_to(0)[0]()
-    weights_to(0)[0]()
-    for c in oh:
-        c.wait()
+    for c in sides:
+        c.wait_recv()
     phase_ocean_rim()
-    rim_to(0)[0]()
+    phase_atm_rim()
     rim_to(1)[0]()
 
     l_tf.wait()
     for c in a1:
         c.wait_recv()
     phase_spectra()
-    ah = []
-    for side, k in ((0, -1), (1, 1)):
-        c = remote(ahs.at[side], ahr.at[side], ahss.at[side], ahrs.at[side], {"col": col_at(k)})
-        c.start()
-        ah.append(c)
     l_ti.wait()
     for k in range(BLOCKS // chunk):
         q = phase_inverse(k)
@@ -619,16 +643,20 @@
 
     recv2[me] = send2[me]
 
+    weights_to(1)[2]()
+    for o in range(2, 6):
+        slots_to(o)[2]()
+    rim_to(0)[0]()
+    weights_to(0)[0]()
+    slots_to(0)[0]()
+    rim_to(1)[2]()
+    phase_stencil(1)
+    weights_to(0)[2]()
     slots_to(0)[2]()
-    weights_to(0)[2]()
     phase_matrices()
     rim_to(0)[2]()
-    rim_to(1)[2]()
-    phase_stencil()
-
-    for c in ah:
-        c.wait()
-    phase_atm_rim()
+    phase_stencil(0)
+
     for k in range(1, cols):
         remote(send2.at[0], recv2.at[0], a2s.at[k], a2r.at[k], {"col": col_at(k)}).wait_recv()
     phase_unpack()
@@ -645,13 +673,15 @@
         flux_to(o)[2]()
     phase_forcing()
     phase_ocean()
-    for o in range(1, SPAN):
+    for o in (3, 2, 1):
         back_to(o)[0]()
     for o in range(1, SPAN):
         back_to(o)[2]()
     phase_sum()
 
     for c in a1:
+        c.wait_send()
+    for c in sides:
         c.wait_send()
     for k in range(1, cols):
         remote(send2.at[0], recv2.at[0], a2s.at[k], a2r.at[k], {"col": col_at(k)}).wait_send()
@@ -697,7 +727,6 @@
     land_mask,
 ):
     any_spec = pl.BlockSpec(memory_space=ANY)
-    smem = pl.BlockSpec(memory_space=pltpu.SMEM)
     vm = pltpu.VMEM
     dma = pltpu.SemaphoreType.DMA
     scratch = [
@@ -722,10 +751,8 @@
         vm((ROWS + 2 * RIM, PAD, HP), F32),
         vm((ROWS, PAD, HP), BF16),
         vm((2, RIM, PAD, HP), BF16),
-        vm((2, ROWS, 8, HP), F32),
-        vm((2, ROWS, 8, HP), F32),
-        vm((2, LATS, 8, CH), F32),
-        vm((2, LATS, 8, CH), F32),
+        vm((2, 16, 2 * HP + CH), BF16),
+        vm((2, 16, 2 * HP + CH), BF16),
         vm((8, 8, 128), F32),
         vm((6, 3, 8, 128), F32),
         vm((8, 128), F32),
@@ -753,15 +780,16 @@
         vm((SPAN, 64, PAD), BF16),
         vm((SPAN, 64, PAD), BF16),
         vm((2, TAB, 128), BF16),
-        dma((15,)),
+        pltpu.SMEM((1, SLOTS, bands), jnp.int32),
+        pltpu.SMEM((1, bands), jnp.int32),
+        pltpu.SMEM((ROWS, SLOTS, bands), F32),
+        dma((18,)),
         dma((16,)),
         dma((16,)),
         dma((16,)),
         dma((16,)),
         dma((6,)),
         dma((6,)),
-        dma((2,)),
-        dma((2,)),
         dma((2,)),
         dma((2,)),
         dma((2,)),
@@ -781,7 +809,7 @@
     out = pl.pallas_call(
         functools.partial(body, bands, cols),
         out_shape=tuple(vm(x.shape, x.dtype) for x in shapes),
-        in_specs=[any_spec] * 5 + [smem] * 3 + [any_spec] * 10,
+        in_specs=[any_spec] * 18,
         out_specs=(pl.BlockSpec(memory_space=vm),) * 3,
         scratch_shapes=scratch,
         compiler_params=pltpu.CompilerParams(
@@ -811,7 +839,7 @@
         in_specs=[pl.BlockSpec(memory_space=vm)] * 3,
         out_specs=(any_spec,) * 3,
         scratch_shapes=[dma((3,))],
-    )(*out)
+    )(*[pltpu.with_memory_space_constraint(x, vm) for x in out])
     return (
         jnp.transpose(out[0], (1, 0, 2)),
         out[1],

time: 42.1 us -> 36.9 us (0.88)
  the two profiles are of different devices: /device:TPU:129 before, /device:TPU:385 now
where the time goes in v3:
time: 36.9 us; the launch traced here: 36.7 us
  Pallas kernels  36.1 us (98%)
  between operations  0.64 us (2%)
    pallas_call x1, Pallas kernels, per_device(): pl.pallas_call(functools.partial(body, bands, cols), out_shape=tuple((vm(...  35.3 us
    pallas_call x1, Pallas kernels, per_device(): pl.pallas_call(store, out_shape=shapes, in_specs=[pl.BlockSpec(memory_spa...  0.84 us

profile of v3, /device:TPU:385, one launch (start us, length us, event | category | flops | bytes accessed | tf_op | source)
XLA Modules:
  0.0 36.7 jit_solution(9491828471705686863)
XLA Ops:
  0.6 35.3 %shard_map.193 = (bf16[90,4,384]{2,1,0:T(4,128)(2,1)S(1)}, bf16[6,90,200]{2,1,0:T(8,128)(2,1)S(1)}, bf16[4,16,90]{2,1,0:T(8,128)(2,1)S(1)}) custom-call(bf16[90,4,384]{2,1,0:T(4,128)(2,1)} %bitcast.11, f32[2,24,720]{2,1,0:T(8,128)} %bitcast.12, bf16[384,768]{1,0:T(8,128)(2,1)} %w_in.1, bf16[768,384]{1,0:T(8,128)(2,1)} %w_out.1, bf16[16,384]{1,0:T(8,128)(2,1)} %bitcast.13, ...), custom_call_target="tpu_custom_call" | custom-call | tf_op jit(solution)/shard_map/pallas_call | solution.py:809
  35.9 0.8 %shard_map.194 = (bf16[90,4,384]{2,1,0:T(4,128)(2,1)}, bf16[6,90,200]{2,1,0:T(8,128)(2,1)}, bf16[4,16,90]{2,1,0:T(8,128)(2,1)}) custom-call(bf16[90,4,384]{2,1,0:T(4,128)(2,1)S(1)} %get-tuple-element.9.a, bf16[6,90,200]{2,1,0:T(8,128)(2,1)S(1)} %get-tuple-element.10.b, bf16[4,16,90]{2,1,0:T(8,128)(2,1)S(1)} %get-tuple-element.11.c), custom_call_target="tpu_custom_call" | custom-call | tf_op jit(solution)/shard_map/pallas_call | solution.py:836

commit v4 on v3

--- a/solution.py
+++ b/solution.py
@@ -21,6 +21,11 @@
 LOCAL = 90
 PAD = 96
 RIM = 3
+MAIN = 80
+TAIL = PAD - MAIN
+FIRST = 48
+REST = MAIN - FIRST
+HEAD = FIRST + TAIL
 KS = 7
 CH = 384
 OWN = 24
@@ -36,12 +41,18 @@
 
 
 def tables():
-    place = np.arange(PAD)
-    block = np.arange(BLOCKS)
-    inside = np.broadcast_to(place < LOCAL, (BLOCKS, PAD)).reshape(-1)
-    lon_in = (LOCAL * block[:, None] + place[None]).reshape(-1)
-    rim = np.where(place < LOCAL + RIM, place, place - PAD)
-    lon_out = (LOCAL * block[:, None] + rim[None]).reshape(-1)
+    block = np.arange(BLOCKS)[:, None]
+
+    def places(*spans):
+        pieces = [(block * LON // 16 + 0 * np.arange(a, b), np.arange(a, b) + 0 * block) for a, b in spans]
+        start = np.concatenate([p[0].reshape(-1) for p in pieces])
+        return start, np.concatenate([p[1].reshape(-1) for p in pieces])
+
+    start, place = places((0, MAIN), (MAIN, PAD))
+    inside = place < LOCAL
+    lon_in = start + place
+    start, place = places((0, FIRST), (MAIN, PAD), (FIRST, MAIN))
+    lon_out = start + np.where(place < LOCAL + RIM, place, place - PAD)
     forward = np.zeros((2, TAB, TAB), np.float64)
     inverse = np.zeros((2, TAB, TAB), np.float64)
     deal = np.zeros((2 * WPAD, TAB), np.float64)
@@ -72,6 +83,27 @@
 
 def dot_nt(a, b):
     return lax.dot_general(a, b, NT, preferred_element_type=F32)
+
+
+def gelu(x):
+    half = 0.5 * x
+    inner = x * (0.7978845608028654 + 0.035677408136300125 * (x * x))
+    return (half + half * jnp.tanh(inner)).astype(BF16)
+
+
+def fold(main, tail, free):
+    return [
+        jnp.where(free, pltpu.roll(tail, 96 - 32 * g, 1), main[TAIL * g : TAIL * g + TAIL])
+        for g in range(3)
+    ]
+
+
+def unfold(main, lane, first):
+    out = None
+    for g in range(3):
+        part = pltpu.roll(main[TAIL * g : TAIL * g + TAIL], 32 + 32 * g, 1)
+        out = part if out is None else jnp.where(((lane - first) & 127) // 32 == g, part, out)
+    return out
 
 
 def windows(tile):
@@ -115,6 +147,10 @@
     recv1,
     send2,
     recv2,
+    send2b,
+    recv2b,
+    tails,
+    tails2,
     tf,
     ti,
     dl,
@@ -152,11 +188,13 @@
     sxt,
     mx,
     nx,
+    flx32,
     flx,
     flr,
     bks,
     bkr,
     waves,
+    sea,
     p_rows,
     p_count,
     p_weight,
@@ -165,6 +203,8 @@
     a1r,
     a2s,
     a2r,
+    a3s,
+    a3r,
     sls,
     slr,
     ws,
@@ -272,6 +312,7 @@
         return to_band(o, bks.at[o], bkr.at[o], bss.at[o], brs.at[o])
 
     lane = iota((PAD, 128), 1)
+    lane16 = iota((TAIL, 128), 1)
 
     def phase_pack():
         st[:, LATS * LOCAL :, :] = jnp.zeros((3, LATS * (PAD - LOCAL), 128), F32)
@@ -292,7 +333,10 @@
                         for a in range(LATS):
                             mask = ((lane - (lo + OWN * a)) & 127) < n
                             out = jnp.where(mask, rolled[a, t], out)
-            send1[d] = out.astype(BF16)
+            free = ((lane16 - OWN * d) & 127) >= 96
+            for g, piece in enumerate(fold(out, out[MAIN:], free)):
+                send1[d, TAIL * g : TAIL * g + TAIL] = piece.astype(BF16)
+            send1[d, FIRST:] = out[FIRST:MAIN].astype(BF16)
         recv1[me] = send1[me]
 
     def phase_slots():
@@ -324,12 +368,12 @@
             @pl.when(jnp.logical_not(exists(o - 1)))
             def _():
                 selr[o] = jnp.zeros((3, 8, 128), F32)
-                flr[o] = jnp.zeros((PAD, 128), BF16)
+                flr[o] = jnp.zeros((FIRST, 128), BF16)
 
         @pl.when(jnp.logical_not(exists(-1)))
         def _():
             selr[0] = jnp.zeros((3, 8, 128), F32)
-            flr[0] = jnp.zeros((PAD, 128), BF16)
+            flr[0] = jnp.zeros((FIRST, 128), BF16)
             wr[0] = zero8
             obr[0] = jnp.zeros((RIM, PAD, HP), BF16)
 
@@ -342,7 +386,7 @@
 
             @pl.when(jnp.logical_not(exists(-o)))
             def _():
-                bkr[o] = jnp.zeros((64, PAD), BF16)
+                bkr[o] = jnp.zeros((FIRST, 128), BF16)
 
     def phase_rims():
         oc[RIM : RIM + ROWS] = jnp.zeros((ROWS, PAD, HP), F32)
@@ -390,7 +434,9 @@
         for dj in range(KS):
             for di in range(KS):
                 at = 128 * dj + FIELDS * di
-                wst[at : at + FIELDS, 0:HO] = (f32_force * kp[di, dj : dj + 1, 0:HO]).astype(BF16)
+                weight = f32_force * kp[di, dj : dj + 1, 0:HO]
+                weight = weight - jnp.mean(weight, axis=-1, keepdims=True)
+                wst[at : at + FIELDS, 0:HO] = weight.astype(BF16)
         fpc[FIELDS * RIM : FIELDS * RIM + FIELDS, 0:HO] = fp[...]
 
         r, f = iota((512, FIELDS), 0), iota((512, FIELDS), 1)
@@ -401,6 +447,8 @@
         sxt[...] = dot(spread, spt[...]).astype(BF16)
         lmp[...] = jnp.zeros(lmp.shape, F32)
         lmp[0:ROWS, 0:LOCAL] = lm[...].astype(F32)
+        r, c_ = iota((128, 128), 0), iota((128, 128), 1)
+        sea[...] = dot_nt(one_hot(r == c_), lmp[...].astype(BF16))
 
     def with_rim(own, right, left, row, k):
         right = pltpu.roll(right, (10 - RIM * k) % 16, 0)
@@ -452,8 +500,16 @@
         bigb[...] = jnp.where(r % 16 == c_ % 16, full, 0.0).astype(BF16)
 
     def phase_spectra():
-        first = recv1[0:BLOCKS].reshape(TAB, 128).astype(F32)
-        second = recv1[BLOCKS : 2 * BLOCKS].reshape(TAB, 128).astype(F32)
+        for j in range(cols):
+            tails[j] = unfold(recv1[j, :FIRST].astype(F32), lane16, OWN * me).astype(BF16)
+
+        def half_circle(k):
+            at = slice(BLOCKS * k, BLOCKS * k + BLOCKS)
+            main = recv1[at].reshape(BLOCKS * MAIN, 128)
+            tail = tails[at].reshape(BLOCKS * TAIL, 128)
+            return jnp.concatenate([main, tail], axis=0).astype(F32)
+
+        first, second = half_circle(0), half_circle(1)
         for parity in range(2):
             mix = first - second if parity else first + second
             spec = dot(tf[parity], mix.astype(BF16))
@@ -463,19 +519,21 @@
             waves[parity, :WPAD] = (g_real * real + g_imag * imag).astype(BF16)
             waves[parity, WPAD:] = (g_real * imag - g_imag * real).astype(BF16)
 
-    chunk = 2
-
-    def phase_inverse(k):
-        parts = BLOCKS // chunk
-        q = lax.rem(me // chunk + k + 1, parts)
-        rows = pl.ds(pl.multiple_of(q * (chunk * PAD), chunk * PAD), chunk * PAD)
-        even = dot(ti[0, rows, :], waves[0])
-        odd = dot(ti[1, rows, :], waves[1])
-        send2[pl.ds(q * chunk, chunk)] = (even + odd).astype(BF16).reshape(chunk, PAD, 128)
-        send2[pl.ds(q * chunk + BLOCKS, chunk)] = (
-            (even - odd).astype(BF16).reshape(chunk, PAD, 128)
-        )
-        return q
+    def phase_inverse(part):
+        low, high = (0, BLOCKS * HEAD) if part == 0 else (BLOCKS * HEAD, TAB)
+        even = dot(ti[0, low:high, :], waves[0])
+        odd = dot(ti[1, low:high, :], waves[1])
+        free = ((lane16 - OWN * me) & 127) >= 96
+        for k, field in enumerate((even + odd, even - odd)):
+            for j in range(BLOCKS):
+                if part:
+                    send2b[BLOCKS * k + j] = field[REST * j : REST * j + REST].astype(BF16)
+                else:
+                    at = BLOCKS * FIRST + TAIL * j
+                    main = field[FIRST * j : FIRST * j + FIRST]
+                    for g, piece in enumerate(fold(main, field[at : at + TAIL], free)):
+                        rows = slice(TAIL * g, TAIL * g + TAIL)
+                        send2[BLOCKS * k + j, rows] = piece.astype(BF16)
 
     def phase_stencil(half):
         if half:
@@ -484,6 +542,7 @@
             oc[0:RIM] = obr[0].astype(F32) * up_ok
 
         def stencil_row(i, carry):
+            totals = []
             for t in range(HP // 128):
                 cut = slice(128 * t, 128 * t + 128)
                 total = None
@@ -495,7 +554,10 @@
                     shift = (RIM - dj) % PAD
                     line = pltpu.roll(line, shift, 0) if shift else line
                     total = line if total is None else total + line
-                s0[i, :, cut] = total
+                totals.append(total)
+            mean = sum(jnp.sum(x, axis=-1, keepdims=True) for x in totals) * (1.0 / HO)
+            for t, total in enumerate(totals):
+                s0[i, :, 128 * t : 128 * t + 128] = total - mean
             return carry
 
         lax.fori_loop(RIM * half, RIM * half + RIM, stencil_row, 0)
@@ -506,47 +568,78 @@
         for a in range(LATS):
             x32[a, 80:96, :] = with_rim(x32[a, 80:96, :], right, left, row, a)
 
-    def phase_unpack():
+    def phase_unpack(part):
+        if part == 0:
+            for d in range(cols):
+                tails2[d] = unfold(recv2[d].astype(F32), lane16, OWN * d)
         for a in range(LATS):
             for t in range(3):
                 cut = slice(128 * t, 128 * t + 128)
-                zonal = jnp.zeros((PAD, 128), F32)
-                for d, lo, n in windows(t):
-                    mask = ((lane - (lo + OWN * a)) & 127) < n
-                    zonal = jnp.where(mask, recv2[d].astype(F32), zonal)
-                if a:
-                    zonal = pltpu.roll(zonal, 128 - OWN * a, 1)
-                mx[a * PAD : a * PAD + PAD, cut] = x32[a, :, cut] + zonal
-
-    def phase_atm():
-        mixed = mx[...]
+
+                def gather(read, rows):
+                    zonal = jnp.zeros((rows, 128), F32)
+                    for d, lo, n in windows(t):
+                        mask = ((lane[:rows] - (lo + OWN * a)) & 127) < n
+                        zonal = jnp.where(mask, read(d), zonal)
+                    return pltpu.roll(zonal, 128 - OWN * a, 1) if a else zonal
+
+                if part == 0:
+                    at = HEAD * a
+                    main = gather(lambda d: recv2[d].astype(F32), FIRST)
+                    mx[at : at + FIRST, cut] = x32[a, :FIRST, cut] + main
+                    tail = gather(lambda d: tails2[d], TAIL)
+                    mx[at + FIRST : at + HEAD, cut] = x32[a, MAIN:, cut] + tail
+                else:
+                    at = LATS * HEAD + REST * a
+                    rest = gather(lambda d: recv2b[d].astype(F32), REST)
+                    mx[at : at + REST, cut] = x32[a, FIRST:MAIN, cut] + rest
+
+    def phase_atm(part):
+        low, n = (0, HEAD) if part == 0 else (LATS * HEAD, REST)
+        rows = slice(low, low + LATS * n)
+        mixed = mx[rows]
         centred = mixed - jnp.mean(mixed, axis=-1, keepdims=True)
         spread = jnp.mean(centred * centred, axis=-1, keepdims=True)
         normed = (centred * lax.rsqrt(spread + 1e-05)).astype(BF16)
-        inner = jax.nn.gelu(dot(normed, w1[...])).astype(BF16)
-        nx[...] = (mx[...] + dot(inner, w2[...])).astype(BF16)
+        inner = gelu(dot(normed, w1[...]))
+        nx[rows] = (mx[rows] + dot(inner, w2[...])).astype(BF16)
         flux = None
         for a in range(LATS):
-            term = dot_nt(nx[a * PAD : a * PAD + PAD, :], fxt[128 * a : 128 * a + 128, :])
+            at = low + n * a
+            term = dot_nt(nx[at : at + n, :], fxt[128 * a : 128 * a + 128, :])
             flux = term if flux is None else flux + term
-        flx[...] = flux.astype(BF16)
-        flr[1] = flx[...]
+        if part == 0:
+            flx32[...] = flux
+        else:
+            lower = iota((FIRST, 128), 1) < 64
+            upper = jnp.concatenate([flux, flx32[FIRST:]], axis=0)
+            flx[...] = jnp.where(lower, flx32[:FIRST], upper).astype(BF16)
+            flr[1] = flx[...]
 
     def phase_atm_out():
         for t in range(3):
             cut = slice(128 * t, 128 * t + 128)
             for a in range(LATS):
-                part = nx[a * PAD : a * PAD + PAD, cut].astype(F32)
-                st.at[t][pl.ds(a, PAD, stride=LATS), :] = part
+                at = HEAD * a
+                rest = LATS * HEAD + REST * a
+                for place, first, n in (
+                    (0, at, FIRST),
+                    (MAIN, at + FIRST, TAIL),
+                    (FIRST, rest, REST),
+                ):
+                    part = nx[first : first + n, cut].astype(F32)
+                    st.at[t][pl.ds(a + LATS * place, n, stride=LATS), :] = part
             for l in range(LOCAL):
                 ao[l, :, cut] = st[t, LATS * l : LATS * l + LATS, :].astype(BF16)
 
     def phase_forcing():
-        low = iota((PAD, 128), 1) < 64
-        tiles = [
-            jnp.where(low, flr[2 * q].astype(F32), flr[2 * q + 1].astype(F32)).astype(BF16)
-            for q in range(3)
-        ]
+        low = iota((FIRST, 128), 1) < 64
+        tiles = []
+        for q in range(3):
+            even, odd = flr[2 * q].astype(F32), flr[2 * q + 1].astype(F32)
+            upper = jnp.where(low, even, pltpu.roll(odd, 64, 1))
+            lower = jnp.where(low, pltpu.roll(even, 64, 1), odd)
+            tiles.append(jnp.concatenate([upper, lower], axis=0).astype(BF16))
         forcing = dot(jnp.concatenate(tiles, axis=1), biga[...])
         for i in range(ROWS):
             part = forcing[:, 128 * i : 128 * i + 128]
@@ -556,14 +649,11 @@
                 xs[PAD * i : PAD * i + PAD, 128 * dj : 128 * dj + 128] = turned.astype(BF16)
 
     def phase_ocean():
-        r, c_ = iota((128, 128), 0), iota((128, 128), 1)
-        sea = dot_nt(one_hot(r == c_), lmp[...].astype(BF16))
         rows = ROWS * PAD
         stencil = (dot(xs[...], wst[...]) + s0[...].reshape(rows, HP))[:, :HO]
-        centred = stencil - jnp.mean(stencil, axis=-1, keepdims=True)
-        spread = jnp.mean(centred * centred, axis=-1, keepdims=True)
-        onorm = (centred * lax.rsqrt(spread + 1e-05)).astype(BF16)
-        hidden = jax.nn.gelu(dot(onorm, oin[...])).astype(BF16)
+        spread = jnp.mean(stencil * stencil, axis=-1, keepdims=True)
+        onorm = (stencil * lax.rsqrt(spread + 1e-05)).astype(BF16)
+        hidden = gelu(dot(onorm, oin[...]))
         change = dot_nt(hidden, oot[...])
         pushed = dot(xs[:, 128 * RIM : 128 * RIM + 128], fpc[...])
         lifted = (oc[RIM : RIM + ROWS].reshape(rows, HP) + pushed)[:, :HO].astype(BF16).astype(F32)
@@ -574,15 +664,19 @@
             oo[i] = part[:LOCAL]
             term = dot_nt(part, sxt[128 * i : 128 * i + 128, :])
             surface = term if surface is None else surface + term
-        back = dot_nt(bigb[...], surface.astype(BF16)).astype(BF16)
+        back = dot_nt(bigb[...], jnp.concatenate([surface.astype(BF16), jnp.zeros((32, 128), BF16)], axis=0))
         for o in range(SPAN):
-            bks[o] = back[64 * o : 64 * o + 64]
+            main, tail = back[64 * o : 64 * o + FIRST], back[64 * o + FIRST : 64 * o + 64]
+            for g, piece in enumerate(fold(main, tail, lane16 >= 96)):
+                bks[o, TAIL * g : TAIL * g + TAIL] = piece.astype(BF16)
 
     def phase_sum():
         total = bks[0].astype(F32)
         for o in range(1, SPAN):
             total = total + bkr[o].astype(F32)
-        so[...] = total.reshape(LATS, FIELDS, PAD)[:, :, :LOCAL].astype(BF16)
+        for a in range(3):
+            so[a] = total[FIELDS * a : FIELDS * a + FIELDS, :LOCAL].astype(BF16)
+        so[3] = unfold(total, lane16, 0)[:, :LOCAL].astype(BF16)
 
     l_atm.wait()
     phase_pack()
@@ -629,19 +723,22 @@
         c.wait_recv()
     phase_spectra()
     l_ti.wait()
-    for k in range(BLOCKS // chunk):
-        q = phase_inverse(k)
-        for n in range(2 * chunk):
-            to = q * chunk + n % chunk + BLOCKS * (n // chunk)
-            step = lax.rem(to - me + cols, cols)
-
-            @pl.when(to != me)
-            def _():
-                remote(
-                    send2.at[to], recv2.at[me], a2s.at[step], a2r.at[step], {"col": to}
-                ).start()
-
+    phase_inverse(0)
+    a2 = []
+    for d in partners:
+        step = lax.rem(d - me + cols, cols)
+        c = remote(send2.at[d], recv2.at[me], a2s.at[step], a2r.at[step], {"col": d})
+        c.start()
+        a2.append(c)
+    phase_inverse(1)
+    a3 = []
+    for d in partners:
+        step = lax.rem(d - me + cols, cols)
+        c = remote(send2b.at[d], recv2b.at[me], a3s.at[step], a3r.at[step], {"col": d})
+        c.start()
+        a3.append(c)
     recv2[me] = send2[me]
+    recv2b[me] = send2b[me]
 
     weights_to(1)[2]()
     for o in range(2, 6):
@@ -657,12 +754,16 @@
     rim_to(0)[2]()
     phase_stencil(0)
 
-    for k in range(1, cols):
-        remote(send2.at[0], recv2.at[0], a2s.at[k], a2r.at[k], {"col": col_at(k)}).wait_recv()
-    phase_unpack()
     l_w1.wait()
     l_w2.wait()
-    phase_atm()
+    for c in a2:
+        c.wait_recv()
+    phase_unpack(0)
+    phase_atm(0)
+    for c in a3:
+        c.wait_recv()
+    phase_unpack(1)
+    phase_atm(1)
     for o in (5, 4, 3, 2, 0):
         flux_to(o)[0]()
     phase_atm_out()
@@ -683,8 +784,8 @@
         c.wait_send()
     for c in sides:
         c.wait_send()
-    for k in range(1, cols):
-        remote(send2.at[0], recv2.at[0], a2s.at[k], a2r.at[k], {"col": col_at(k)}).wait_send()
+    for c in a2 + a3:
+        c.wait_send()
     for o in (0, 2, 3, 4, 5):
         slots_to(o)[1]()
         flux_to(o)[1]()
@@ -734,10 +835,14 @@
         vm((3, LATS * PAD, 128), F32),
         vm((LATS, PAD, CH), F32),
         vm((LATS, 3, PAD, 128), F32),
-        vm((16, PAD, 128), BF16),
-        vm((16, PAD, 128), BF16),
-        vm((16, PAD, 128), BF16),
-        vm((16, PAD, 128), BF16),
+        vm((16, MAIN, 128), BF16),
+        vm((16, MAIN, 128), BF16),
+        vm((16, FIRST, 128), BF16),
+        vm((16, FIRST, 128), BF16),
+        vm((16, REST, 128), BF16),
+        vm((16, REST, 128), BF16),
+        vm((16, TAIL, 128), BF16),
+        vm((16, TAIL, 128), F32),
         vm((2, TAB, TAB), BF16),
         vm((2, TAB, TAB), BF16),
         vm((TAB, TAB), BF16),
@@ -775,15 +880,19 @@
         vm((768, HO), BF16),
         vm((LATS * PAD, CH), F32),
         vm((LATS * PAD, CH), BF16),
-        vm((PAD, 128), BF16),
-        vm((6, PAD, 128), BF16),
-        vm((SPAN, 64, PAD), BF16),
-        vm((SPAN, 64, PAD), BF16),
+        vm((HEAD, 128), F32),
+        vm((FIRST, 128), BF16),
+        vm((6, FIRST, 128), BF16),
+        vm((SPAN, FIRST, 128), BF16),
+        vm((SPAN, FIRST, 128), BF16),
         vm((2, TAB, 128), BF16),
+        vm((128, 8), F32),
         pltpu.SMEM((1, SLOTS, bands), jnp.int32),
         pltpu.SMEM((1, bands), jnp.int32),
         pltpu.SMEM((ROWS, SLOTS, bands), F32),
         dma((18,)),
+        dma((16,)),
+        dma((16,)),
         dma((16,)),
         dma((16,)),
         dma((16,)),

time: 36.9 us -> 36.6 us (level)
  no operation moved by 1% of the time
where the time goes in v4:
time: 36.6 us; the launch traced here: 36.4 us
  Pallas kernels  35.8 us (98%)
  between operations  0.64 us (2%)
    pallas_call x1, Pallas kernels, per_device(): pl.pallas_call(functools.partial(body, bands, cols), out_shape=tuple((vm(...  35 us
    pallas_call x1, Pallas kernels, per_device(): pl.pallas_call(store, out_shape=shapes, in_specs=[pl.BlockSpec(memory_spa...  0.84 us

profile of v4, /device:TPU:385, one launch (start us, length us, event | category | flops | bytes accessed | tf_op | source)
XLA Modules:
  0.0 36.4 jit_solution(12237858571328919230)
XLA Ops:
  0.6 35.0 %shard_map.193 = (bf16[90,4,384]{2,1,0:T(4,128)(2,1)S(1)}, bf16[6,90,200]{2,1,0:T(8,128)(2,1)S(1)}, bf16[4,16,90]{2,1,0:T(8,128)(2,1)S(1)}) custom-call(bf16[90,4,384]{2,1,0:T(4,128)(2,1)} %bitcast.11, f32[2,24,720]{2,1,0:T(8,128)} %bitcast.12, bf16[384,768]{1,0:T(8,128)(2,1)} %w_in.1, bf16[768,384]{1,0:T(8,128)(2,1)} %w_out.1, bf16[16,384]{1,0:T(8,128)(2,1)} %bitcast.13, ...), custom_call_target="tpu_custom_call" | custom-call | tf_op jit(solution)/shard_map/pallas_call | solution.py:918
  35.6 0.8 %shard_map.194 = (bf16[90,4,384]{2,1,0:T(4,128)(2,1)}, bf16[6,90,200]{2,1,0:T(8,128)(2,1)}, bf16[4,16,90]{2,1,0:T(8,128)(2,1)}) custom-call(bf16[90,4,384]{2,1,0:T(4,128)(2,1)S(1)} %get-tuple-element.9.a, bf16[6,90,200]{2,1,0:T(8,128)(2,1)S(1)} %get-tuple-element.10.b, bf16[4,16,90]{2,1,0:T(8,128)(2,1)S(1)} %get-tuple-element.11.c), custom_call_target="tpu_custom_call" | custom-call | tf_op jit(solution)/shard_map/pallas_call | solution.py:945

commit v5 on v4

--- a/solution.py
+++ b/solution.py
@@ -188,7 +188,6 @@
     sxt,
     mx,
     nx,
-    flx32,
     flx,
     flr,
     bks,
@@ -243,6 +242,15 @@
         return c
 
     l_atm = load(atm, xv, 0)
+    barrier = pltpu.get_barrier_semaphore()
+    for d in partners:
+        pl.semaphore_signal(barrier, inc=1, device_id={"col": d}, device_id_type=MESH)
+    for k in range(1, SPAN + 1):
+
+        @pl.when(exists(k))
+        def _():
+            pl.semaphore_signal(barrier, inc=1, device_id={"band": band + k}, device_id_type=MESH)
+
     l_rows = load(pair_rows, p_rows, 15)
     l_count = load(pair_count, p_count, 16)
     l_weight = load(pair_weight, p_weight, 17)
@@ -260,15 +268,6 @@
     l_w2 = load(w_out, w2, 12)
     l_oin = load(o_in, oin, 13)
     l_oot = load(o_out_t, oot, 14)
-
-    barrier = pltpu.get_barrier_semaphore()
-    for d in partners:
-        pl.semaphore_signal(barrier, inc=1, device_id={"col": d}, device_id_type=MESH)
-    for k in range(1, SPAN + 1):
-
-        @pl.when(exists(k))
-        def _():
-            pl.semaphore_signal(barrier, inc=1, device_id={"band": band + k}, device_id_type=MESH)
 
     def remote(src, dst, send_sem, recv_sem, device):
         return pltpu.make_async_remote_copy(
@@ -594,27 +593,23 @@
                     rest = gather(lambda d: recv2b[d].astype(F32), REST)
                     mx[at : at + REST, cut] = x32[a, FIRST:MAIN, cut] + rest
 
-    def phase_atm(part):
-        low, n = (0, HEAD) if part == 0 else (LATS * HEAD, REST)
-        rows = slice(low, low + LATS * n)
-        mixed = mx[rows]
+    def phase_atm():
+        mixed = mx[...]
         centred = mixed - jnp.mean(mixed, axis=-1, keepdims=True)
         spread = jnp.mean(centred * centred, axis=-1, keepdims=True)
         normed = (centred * lax.rsqrt(spread + 1e-05)).astype(BF16)
         inner = gelu(dot(normed, w1[...]))
-        nx[rows] = (mx[rows] + dot(inner, w2[...])).astype(BF16)
+        nx[...] = (mx[...] + dot(inner, w2[...])).astype(BF16)
         flux = None
         for a in range(LATS):
-            at = low + n * a
-            term = dot_nt(nx[at : at + n, :], fxt[128 * a : 128 * a + 128, :])
+            near, rest = HEAD * a, LATS * HEAD + REST * a
+            rows = jnp.concatenate([nx[near : near + HEAD], nx[rest : rest + REST]], axis=0)
+            term = dot_nt(rows, fxt[128 * a : 128 * a + 128, :])
             flux = term if flux is None else flux + term
-        if part == 0:
-            flx32[...] = flux
-        else:
-            lower = iota((FIRST, 128), 1) < 64
-            upper = jnp.concatenate([flux, flx32[FIRST:]], axis=0)
-            flx[...] = jnp.where(lower, flx32[:FIRST], upper).astype(BF16)
-            flr[1] = flx[...]
+        lower = iota((FIRST, 128), 1) < 64
+        upper = jnp.concatenate([flux[HEAD:], flux[FIRST:HEAD]], axis=0)
+        flx[...] = jnp.where(lower, flux[:FIRST], upper).astype(BF16)
+        flr[1] = flx[...]
 
     def phase_atm_out():
         for t in range(3):
@@ -680,12 +675,6 @@
 
     l_atm.wait()
     phase_pack()
-    l_rows.wait()
-    l_count.wait()
-    l_weight.wait()
-    phase_slots()
-    l_ocean.wait()
-    phase_rims()
     pl.semaphore_wait(barrier, cols - 1 + jnp.minimum(band, SPAN))
 
     a1 = []
@@ -694,15 +683,20 @@
         c = remote(send1.at[d], recv1.at[me], a1s.at[step], a1r.at[step], {"col": d})
         c.start()
         a1.append(c)
+    l_rows.wait()
+    l_count.wait()
+    l_weight.wait()
+    phase_slots()
+    weights_to(1)[0]()
+    for o in range(2, 6):
+        slots_to(o)[0]()
+    l_ocean.wait()
+    phase_rims()
     sides = []
     for side, k in ((0, -1), (1, 1)):
         c = remote(side_s.at[side], side_r.at[side], sds.at[side], sdr.at[side], {"col": col_at(k)})
         c.start()
         sides.append(c)
-    weights_to(1)[0]()
-    for o in range(2, 6):
-        slots_to(o)[0]()
-
     l_gain.wait()
     l_deal.wait()
     phase_gains()
@@ -715,8 +709,12 @@
     for c in sides:
         c.wait_recv()
     phase_ocean_rim()
+    rim_to(1)[0]()
+    weights_to(1)[2]()
+    rim_to(0)[0]()
+    weights_to(0)[0]()
+    slots_to(0)[0]()
     phase_atm_rim()
-    rim_to(1)[0]()
 
     l_tf.wait()
     for c in a1:
@@ -740,17 +738,8 @@
     recv2[me] = send2[me]
     recv2b[me] = send2b[me]
 
-    weights_to(1)[2]()
-    for o in range(2, 6):
-        slots_to(o)[2]()
-    rim_to(0)[0]()
-    weights_to(0)[0]()
-    slots_to(0)[0]()
     rim_to(1)[2]()
     phase_stencil(1)
-    weights_to(0)[2]()
-    slots_to(0)[2]()
-    phase_matrices()
     rim_to(0)[2]()
     phase_stencil(0)
 
@@ -759,14 +748,17 @@
     for c in a2:
         c.wait_recv()
     phase_unpack(0)
-    phase_atm(0)
     for c in a3:
         c.wait_recv()
     phase_unpack(1)
-    phase_atm(1)
+    phase_atm()
     for o in (5, 4, 3, 2, 0):
         flux_to(o)[0]()
     phase_atm_out()
+    for o in (0, 2, 3, 4, 5):
+        slots_to(o)[2]()
+    weights_to(0)[2]()
+    phase_matrices()
 
     l_oin.wait()
     l_oot.wait()
@@ -880,7 +872,6 @@
         vm((768, HO), BF16),
         vm((LATS * PAD, CH), F32),
         vm((LATS * PAD, CH), BF16),
-        vm((HEAD, 128), F32),
         vm((FIRST, 128), BF16),
         vm((6, FIRST, 128), BF16),
         vm((SPAN, FIRST, 128), BF16),

time: 36.6 us -> 36 us (0.984)
  the two profiles are of different devices: /device:TPU:385 before, /device:TPU:98 now
where the time goes in v5:
time: 36 us; the launch traced here: 35.9 us
  Pallas kernels  35.2 us (98%)
  between operations  0.64 us (2%)
    pallas_call x1, Pallas kernels, per_device(): pl.pallas_call(functools.partial(body, bands, cols), out_shape=tuple((vm(...  34.4 us
    pallas_call x1, Pallas kernels, per_device(): pl.pallas_call(store, out_shape=shapes, in_specs=[pl.BlockSpec(memory_spa...  0.84 us

profile of v5, /device:TPU:98, one launch (start us, length us, event | category | flops | bytes accessed | tf_op | source)
XLA Modules:
  0.0 35.9 jit_solution(5543808070257125108)
XLA Ops:
  0.6 34.4 %shard_map.193 = (bf16[90,4,384]{2,1,0:T(4,128)(2,1)S(1)}, bf16[6,90,200]{2,1,0:T(8,128)(2,1)S(1)}, bf16[4,16,90]{2,1,0:T(8,128)(2,1)S(1)}) custom-call(bf16[90,4,384]{2,1,0:T(4,128)(2,1)} %bitcast.11, f32[2,24,720]{2,1,0:T(8,128)} %bitcast.12, bf16[384,768]{1,0:T(8,128)(2,1)} %w_in.1, bf16[768,384]{1,0:T(8,128)(2,1)} %w_out.1, bf16[16,384]{1,0:T(8,128)(2,1)} %bitcast.13, ...), custom_call_target="tpu_custom_call" | custom-call | tf_op jit(solution)/shard_map/pallas_call | solution.py:909
  35.0 0.8 %shard_map.194 = (bf16[90,4,384]{2,1,0:T(4,128)(2,1)}, bf16[6,90,200]{2,1,0:T(8,128)(2,1)}, bf16[4,16,90]{2,1,0:T(8,128)(2,1)}) custom-call(bf16[90,4,384]{2,1,0:T(4,128)(2,1)S(1)} %get-tuple-element.9.a, bf16[6,90,200]{2,1,0:T(8,128)(2,1)S(1)} %get-tuple-element.10.b, bf16[4,16,90]{2,1,0:T(8,128)(2,1)S(1)} %get-tuple-element.11.c), custom_call_target="tpu_custom_call" | custom-call | tf_op jit(solution)/shard_map/pallas_call | solution.py:936

commit v6 on v5

--- a/solution.py
+++ b/solution.py
@@ -43,7 +43,7 @@
 def tables():
     block = np.arange(BLOCKS)[:, None]
 
-    def places(*spans):
+    def places(*spans, block=block):
         pieces = [(block * LON // 16 + 0 * np.arange(a, b), np.arange(a, b) + 0 * block) for a, b in spans]
         start = np.concatenate([p[0].reshape(-1) for p in pieces])
         return start, np.concatenate([p[1].reshape(-1) for p in pieces])
@@ -51,7 +51,9 @@
     start, place = places((0, MAIN), (MAIN, PAD))
     inside = place < LOCAL
     lon_in = start + place
-    start, place = places((0, FIRST), (MAIN, PAD), (FIRST, MAIN))
+    spans = ((0, FIRST), (MAIN, PAD), (FIRST, MAIN))
+    halves = [places(*spans, block=block[h : h + BLOCKS // 2]) for h in (0, BLOCKS // 2)]
+    start, place = [np.concatenate([half[n] for half in halves]) for n in range(2)]
     lon_out = start + np.where(place < LOCAL + RIM, place, place - PAD)
     forward = np.zeros((2, TAB, TAB), np.float64)
     inverse = np.zeros((2, TAB, TAB), np.float64)
@@ -147,8 +149,6 @@
     recv1,
     send2,
     recv2,
-    send2b,
-    recv2b,
     tails,
     tails2,
     tf,
@@ -202,8 +202,6 @@
     a1r,
     a2s,
     a2r,
-    a3s,
-    a3r,
     sls,
     slr,
     ws,
@@ -518,21 +516,22 @@
             waves[parity, :WPAD] = (g_real * real + g_imag * imag).astype(BF16)
             waves[parity, WPAD:] = (g_real * imag - g_imag * real).astype(BF16)
 
-    def phase_inverse(part):
-        low, high = (0, BLOCKS * HEAD) if part == 0 else (BLOCKS * HEAD, TAB)
-        even = dot(ti[0, low:high, :], waves[0])
-        odd = dot(ti[1, low:high, :], waves[1])
+    def phase_inverse(k):
+        each = BLOCKS // 2
+        q = lax.rem(me // 4 + k + 1, 2)
+        at = pl.ds(pl.multiple_of(q * (each * PAD), each * PAD), each * PAD)
+        even = dot(ti[0, at, :], waves[0])
+        odd = dot(ti[1, at, :], waves[1])
         free = ((lane16 - OWN * me) & 127) >= 96
-        for k, field in enumerate((even + odd, even - odd)):
-            for j in range(BLOCKS):
-                if part:
-                    send2b[BLOCKS * k + j] = field[REST * j : REST * j + REST].astype(BF16)
-                else:
-                    at = BLOCKS * FIRST + TAIL * j
-                    main = field[FIRST * j : FIRST * j + FIRST]
-                    for g, piece in enumerate(fold(main, field[at : at + TAIL], free)):
-                        rows = slice(TAIL * g, TAIL * g + TAIL)
-                        send2[BLOCKS * k + j, rows] = piece.astype(BF16)
+        for n, field in enumerate((even + odd, even - odd)):
+            for j in range(each):
+                to = BLOCKS * n + each * q + j
+                tail = each * FIRST + TAIL * j
+                rest = each * HEAD + REST * j
+                main = field[FIRST * j : FIRST * j + FIRST]
+                for g, piece in enumerate(fold(main, field[tail : tail + TAIL], free)):
+                    send2[to, TAIL * g : TAIL * g + TAIL] = piece.astype(BF16)
+                send2[to, FIRST:] = field[rest : rest + REST].astype(BF16)
 
     def phase_stencil(half):
         if half:
@@ -570,7 +569,7 @@
     def phase_unpack(part):
         if part == 0:
             for d in range(cols):
-                tails2[d] = unfold(recv2[d].astype(F32), lane16, OWN * d)
+                tails2[d] = unfold(recv2[d, :FIRST].astype(F32), lane16, OWN * d)
         for a in range(LATS):
             for t in range(3):
                 cut = slice(128 * t, 128 * t + 128)
@@ -584,13 +583,13 @@
 
                 if part == 0:
                     at = HEAD * a
-                    main = gather(lambda d: recv2[d].astype(F32), FIRST)
+                    main = gather(lambda d: recv2[d, :FIRST].astype(F32), FIRST)
                     mx[at : at + FIRST, cut] = x32[a, :FIRST, cut] + main
                     tail = gather(lambda d: tails2[d], TAIL)
                     mx[at + FIRST : at + HEAD, cut] = x32[a, MAIN:, cut] + tail
                 else:
                     at = LATS * HEAD + REST * a
-                    rest = gather(lambda d: recv2b[d].astype(F32), REST)
+                    rest = gather(lambda d: recv2[d, FIRST:].astype(F32), REST)
                     mx[at : at + REST, cut] = x32[a, FIRST:MAIN, cut] + rest
 
     def phase_atm():
@@ -721,22 +720,18 @@
         c.wait_recv()
     phase_spectra()
     l_ti.wait()
-    phase_inverse(0)
     a2 = []
-    for d in partners:
-        step = lax.rem(d - me + cols, cols)
-        c = remote(send2.at[d], recv2.at[me], a2s.at[step], a2r.at[step], {"col": d})
-        c.start()
-        a2.append(c)
-    phase_inverse(1)
-    a3 = []
-    for d in partners:
-        step = lax.rem(d - me + cols, cols)
-        c = remote(send2b.at[d], recv2b.at[me], a3s.at[step], a3r.at[step], {"col": d})
-        c.start()
-        a3.append(c)
+    for k, across in enumerate(((1, 3), (2, 0))):
+        phase_inverse(k)
+        for dy in across:
+            for dx in (2, 1, 3, 0):
+                if dy or dx:
+                    d = lax.rem(me // 4 + dy, 4) * 4 + lax.rem(me % 4 + dx, 4)
+                    step = lax.rem(d - me + cols, cols)
+                    c = remote(send2.at[d], recv2.at[me], a2s.at[step], a2r.at[step], {"col": d})
+                    c.start()
+                    a2.append(c)
     recv2[me] = send2[me]
-    recv2b[me] = send2b[me]
 
     rim_to(1)[2]()
     phase_stencil(1)
@@ -748,8 +743,6 @@
     for c in a2:
         c.wait_recv()
     phase_unpack(0)
-    for c in a3:
-        c.wait_recv()
     phase_unpack(1)
     phase_atm()
     for o in (5, 4, 3, 2, 0):
@@ -776,7 +769,7 @@
         c.wait_send()
     for c in sides:
         c.wait_send()
-    for c in a2 + a3:
+    for c in a2:
         c.wait_send()
     for o in (0, 2, 3, 4, 5):
         slots_to(o)[1]()
@@ -829,10 +822,8 @@
         vm((LATS, 3, PAD, 128), F32),
         vm((16, MAIN, 128), BF16),
         vm((16, MAIN, 128), BF16),
-        vm((16, FIRST, 128), BF16),
-        vm((16, FIRST, 128), BF16),
-        vm((16, REST, 128), BF16),
-        vm((16, REST, 128), BF16),
+        vm((16, MAIN, 128), BF16),
+        vm((16, MAIN, 128), BF16),
         vm((16, TAIL, 128), BF16),
         vm((16, TAIL, 128), F32),
         vm((2, TAB, TAB), BF16),
@@ -882,8 +873,6 @@
         pltpu.SMEM((1, bands), jnp.int32),
         pltpu.SMEM((ROWS, SLOTS, bands), F32),
         dma((18,)),
-        dma((16,)),
-        dma((16,)),
         dma((16,)),
         dma((16,)),
         dma((16,)),

time: 36 us -> 35.4 us (0.983)
  the two profiles are of different devices: /device:TPU:98 before, /device:TPU:96 now
where the time goes in v6:
time: 35.4 us; the launch traced here: 35.2 us
  Pallas kernels  34.6 us (98%)
  between operations  0.64 us (2%)
    pallas_call x1, Pallas kernels, per_device(): pl.pallas_call(functools.partial(body, bands, cols), out_shape=tuple((vm(...  33.8 us
    pallas_call x1, Pallas kernels, per_device(): pl.pallas_call(store, out_shape=shapes, in_specs=[pl.BlockSpec(memory_spa...  0.84 us

profile of v6, /device:TPU:96, one launch (start us, length us, event | category | flops | bytes accessed | tf_op | source)
XLA Modules:
  0.0 35.2 jit_solution(3504549626709586172)
XLA Ops:
  0.6 33.8 %shard_map.193 = (bf16[90,4,384]{2,1,0:T(4,128)(2,1)S(1)}, bf16[6,90,200]{2,1,0:T(8,128)(2,1)S(1)}, bf16[4,16,90]{2,1,0:T(8,128)(2,1)S(1)}) custom-call(bf16[90,4,384]{2,1,0:T(4,128)(2,1)} %bitcast.11, f32[2,24,720]{2,1,0:T(8,128)} %bitcast.12, bf16[384,768]{1,0:T(8,128)(2,1)} %w_in.1, bf16[768,384]{1,0:T(8,128)(2,1)} %w_out.1, bf16[16,384]{1,0:T(8,128)(2,1)} %bitcast.13, ...), custom_call_target="tpu_custom_call" | custom-call | tf_op jit(solution)/shard_map/pallas_call | solution.py:898
  34.4 0.8 %shard_map.194 = (bf16[90,4,384]{2,1,0:T(4,128)(2,1)}, bf16[6,90,200]{2,1,0:T(8,128)(2,1)}, bf16[4,16,90]{2,1,0:T(8,128)(2,1)}) custom-call(bf16[90,4,384]{2,1,0:T(4,128)(2,1)S(1)} %get-tuple-element.9.a, bf16[6,90,200]{2,1,0:T(8,128)(2,1)S(1)} %get-tuple-element.10.b, bf16[4,16,90]{2,1,0:T(8,128)(2,1)S(1)} %get-tuple-element.11.c), custom_call_target="tpu_custom_call" | custom-call | tf_op jit(solution)/shard_map/pallas_call | solution.py:925
